TPU v7x, 128 devices: a whole 4x4x4 slice. The times are simulated.
128 devices in a mesh: head: 4 (over z), blk: 32 (over y, x, core).
Axes of the slice: x: 4, y: 4, z: 4, core: 2. Of those that a mesh axis runs over, the one named last changes fastest.
Arguments:
- tokens: bfloat16 [32, 512, 2048], P('blk', 'head'), may hold values from -6 to 6
- segments: int32 [32, 512], replicated, may hold values from 0 to 15, as said below
- w_query: bfloat16 [2048, 2048], P('blk', 'head'), may hold values from -0.125 to 0.125
- key_projection: bfloat16 [2048, 256], P('blk', 'head'), may hold values from -0.125 to 0.125
- value_projection: bfloat16 [2048, 256], P('blk', 'head'), may hold values from -0.125 to 0.125
- w_out: bfloat16 [2048, 2048], P('head', 'blk'), may hold values from -1.5 to 1.5
- w_gate: bfloat16 [2048, 5632], P('blk', 'head'), may hold values from -0.125 to 0.125
- w_up: bfloat16 [2048, 5632], P('blk', 'head'), may hold values from -0.125 to 0.125
- w_down: bfloat16 [5632, 2048], P('head', 'blk'), may hold values from -0.078125 to 0.078125
- norm_attn: bfloat16 [2048], replicated, may hold values from 0.099609375 to 1.8984375
- norm_ffn: bfloat16 [2048], replicated, may hold values from 0.099609375 to 1.8984375
- cotangent: bfloat16 [32, 512, 2048], P('blk', 'head'), may hold values from -6 to 6
Outputs:
- output: bfloat16 [32, 512, 2048], P('blk', 'head')
- grad_tokens: bfloat16 [32, 512, 2048], P('blk', 'head')
- grad_w_query: float32 [2048, 2048], P('blk', 'head')
- grad_w_key: float32 [2048, 256], P('blk', 'head')
- grad_w_value: float32 [2048, 256], P('blk', 'head')
- grad_w_out: float32 [2048, 2048], P('head', 'blk')
- grad_w_gate: float32 [2048, 5632], P('blk', 'head')
- grad_w_up: float32 [2048, 5632], P('blk', 'head')
- grad_w_down: float32 [5632, 2048], P('head', 'blk')
- grad_norm_attn: float32 [2048], replicated
- grad_norm_ffn: float32 [2048], replicated
Inputs may be any that keep to these rules, and one draw needn't show every extreme that they name: `segments`: read in order of blocks and rows, the document numbers never fall; they begin at 0 and end at 15.
All inputs are finite; a program needn't handle non-finite values.
Results may differ from a plain program's by a relative error of at most 0.025.
Values may be sent and summed in bfloat16 or wider, within the bound.
No kernel may reach another device: no remote copies, remote signals or barrier semaphores. Data moves between devices by JAX's collectives and lax.ppermute only.
A program may use at most 192 MiB of HBM per device.

v0:
```python
import jax
import jax.numpy as jnp
from jax import lax
from jax.sharding import PartitionSpec as P

HEAD_SIZE = 64
WINDOW = 1024


epsilon = 1e-05


def from_behind(block, axis, distance):
    devices = range(lax.axis_size(axis))
    route = [(i - distance, i) for i in devices if i - distance in devices]
    return lax.ppermute(block, axis, route)


def matrix_multiply(former, latter):
    return jnp.dot(former, latter, preferred_element_type=jnp.float32)


def matmul_nt(former, latter):
    return lax.dot_general(
        former, latter, (((1,), (1,)), ((), ())), preferred_element_type=jnp.float32
    )


def matmul_tn(former, latter):
    return lax.dot_general(
        former, latter, (((0,), (0,)), ((), ())), preferred_element_type=jnp.float32
    )


def norm_forward(value_vectors, gain_vector):
    inv_root = lax.rsqrt(jnp.mean(value_vectors * value_vectors, -1, keepdims=True) + epsilon)
    return (value_vectors * inv_root * gain_vector, inv_root)


def norm_backward(value_vectors, inv_root, gain_vector, grad_normed):
    weighted = grad_normed * gain_vector
    inner = jnp.mean(weighted * value_vectors, -1, keepdims=True)
    return inv_root * weighted - value_vectors * inv_root * inv_root * inv_root * inner


def gain_term(value_vectors, inv_root, grad_normed):
    return jnp.sum(grad_normed * value_vectors * inv_root, 0)


def rotary_tables(token_positions):
    half_size = HEAD_SIZE // 2
    frequency = 10000.0 ** (-jnp.arange(half_size, dtype=jnp.float32) * 2.0 / HEAD_SIZE)
    angles = token_positions.astype(jnp.float32)[:, None] * frequency[None, :]
    return (jnp.cos(angles), jnp.sin(angles))


def apply_rotary(value_vectors, cosine_table, sine_table, head_count, direction):
    shaped = value_vectors.reshape(value_vectors.shape[0], head_count, HEAD_SIZE)
    half_size = HEAD_SIZE // 2
    first_half = shaped[..., :half_size]
    second_half = shaped[..., half_size:]
    cosine_part = cosine_table[:, None, :]
    sine_part = direction * sine_table[:, None, :]
    rotated = jnp.concatenate(
        [
            first_half * cosine_part - second_half * sine_part,
            second_half * cosine_part + first_half * sine_part,
        ],
        -1,
    )
    return rotated.reshape(value_vectors.shape)


def head_scores(query_head, key_head, mask_table):
    scores = matmul_nt(query_head, key_head) * HEAD_SIZE ** (-0.5)
    return jnp.where(mask_table, scores, -jnp.inf)


def attend(queries, keys_all, mask_table, query_heads, kv_heads):
    heads_per_group = query_heads // kv_heads
    block_rows = queries.shape[0]

    def one_head(head_number, state_pair):
        outputs, logsum = state_pair
        kv_number = head_number // heads_per_group
        query_head = lax.dynamic_slice_in_dim(queries, head_number * HEAD_SIZE, HEAD_SIZE, 1)
        key_head = lax.dynamic_slice_in_dim(keys_all, kv_number * HEAD_SIZE, HEAD_SIZE, 1)
        value_head = lax.dynamic_slice_in_dim(
            keys_all, (kv_heads + kv_number) * HEAD_SIZE, HEAD_SIZE, 1
        )
        scores = head_scores(query_head, key_head, mask_table)
        maximum = jnp.max(scores, -1, keepdims=True)
        exponents = jnp.exp(scores - maximum)
        totals = jnp.sum(exponents, -1, keepdims=True)
        probabilities = (exponents / totals).astype(jnp.bfloat16)
        result = matrix_multiply(probabilities, value_head).astype(jnp.bfloat16)
        outputs = lax.dynamic_update_slice_in_dim(outputs, result, head_number * HEAD_SIZE, 1)
        logsum = lax.dynamic_update_slice_in_dim(
            logsum, (maximum + jnp.log(totals)).T, head_number, 0
        )
        return (outputs, logsum)

    initial = (
        jnp.zeros((block_rows, query_heads * HEAD_SIZE), jnp.bfloat16),
        jnp.zeros((query_heads, block_rows), jnp.float32),
    )
    return lax.fori_loop(0, query_heads, one_head, initial)


def attend_back(queries, keys_all, mask_table, logsum, grad_attended, query_heads, kv_heads):
    heads_per_group = query_heads // kv_heads
    block_rows = queries.shape[0]
    scale_factor = HEAD_SIZE ** (-0.5)

    def one_head(head_number, state_pair):
        grad_queries, grad_keys = state_pair
        kv_number = head_number // heads_per_group
        query_head = lax.dynamic_slice_in_dim(queries, head_number * HEAD_SIZE, HEAD_SIZE, 1)
        key_head = lax.dynamic_slice_in_dim(keys_all, kv_number * HEAD_SIZE, HEAD_SIZE, 1)
        value_head = lax.dynamic_slice_in_dim(
            keys_all, (kv_heads + kv_number) * HEAD_SIZE, HEAD_SIZE, 1
        )
        grad_head = lax.dynamic_slice_in_dim(grad_attended, head_number * HEAD_SIZE, HEAD_SIZE, 1)
        scores = head_scores(query_head, key_head, mask_table)
        row_logsum = lax.dynamic_index_in_dim(logsum, head_number, 0, keepdims=False)
        probabilities = jnp.exp(scores - row_logsum[:, None])
        grad_probs = matmul_nt(grad_head, value_head)
        inner = jnp.sum(probabilities * grad_probs, -1, keepdims=True)
        grad_scores = (probabilities * (grad_probs - inner)).astype(jnp.bfloat16)
        grad_query = matrix_multiply(grad_scores, key_head) * scale_factor
        grad_key = matmul_tn(grad_scores, query_head) * scale_factor
        grad_value = matmul_tn(probabilities.astype(jnp.bfloat16), grad_head)
        grad_queries = lax.dynamic_update_slice_in_dim(
            grad_queries, grad_query, head_number * HEAD_SIZE, 1
        )
        old_key = lax.dynamic_slice_in_dim(grad_keys, kv_number * HEAD_SIZE, HEAD_SIZE, 1)
        grad_keys = lax.dynamic_update_slice_in_dim(
            grad_keys, old_key + grad_key, kv_number * HEAD_SIZE, 1
        )
        old_value = lax.dynamic_slice_in_dim(
            grad_keys, (kv_heads + kv_number) * HEAD_SIZE, HEAD_SIZE, 1
        )
        grad_keys = lax.dynamic_update_slice_in_dim(
            grad_keys, old_value + grad_value, (kv_heads + kv_number) * HEAD_SIZE, 1
        )
        return (grad_queries, grad_keys)

    initial = (
        jnp.zeros((block_rows, query_heads * HEAD_SIZE), jnp.float32),
        jnp.zeros((keys_all.shape[0], 2 * kv_heads * HEAD_SIZE), jnp.float32),
    )
    return lax.fori_loop(0, query_heads, one_head, initial)


def per_device(
    tokens,
    segments,
    w_query,
    key_projection,
    value_projection,
    w_out,
    w_gate,
    w_up,
    w_down,
    norm_attn,
    norm_ffn,
    cotangent,
):
    head_total = lax.axis_size("head")
    head_index = lax.axis_index("head")
    block_index = lax.axis_index("blk")
    local_rows = tokens.shape[1]
    block_rows = local_rows * head_total
    reach = (WINDOW + block_rows - 2) // block_rows
    own_offset = head_index * local_rows
    query_full, key_full, value_full, out_full, gate_part, up_part, down_part = (
        lax.all_gather(w_query, "blk", axis=0, tiled=True),
        lax.all_gather(key_projection, "blk", axis=0, tiled=True),
        lax.all_gather(value_projection, "blk", axis=0, tiled=True),
        lax.all_gather(w_out, "blk", axis=1, tiled=True),
        lax.all_gather(w_gate, "blk", axis=0, tiled=True),
        lax.all_gather(w_up, "blk", axis=0, tiled=True),
        lax.all_gather(w_down, "blk", axis=1, tiled=True),
    )
    query_heads = query_full.shape[1] // HEAD_SIZE
    kv_heads = key_full.shape[1] // HEAD_SIZE
    gain_one = norm_attn.astype(jnp.float32)
    gain_two = norm_ffn.astype(jnp.float32)
    block_tokens = lax.all_gather(tokens[0], "head", axis=0, tiled=True)
    block_float = block_tokens.astype(jnp.float32)
    first_normed, scale_one = norm_forward(block_float, gain_one)
    normed_low = first_normed.astype(jnp.bfloat16)
    token_positions = block_index * block_rows + jnp.arange(block_rows, dtype=jnp.int32)
    cosine_table, sine_table = rotary_tables(token_positions)
    queries = apply_rotary(
        matrix_multiply(normed_low, query_full), cosine_table, sine_table, query_heads, 1.0
    ).astype(jnp.bfloat16)
    keys_own = apply_rotary(
        matrix_multiply(normed_low, key_full), cosine_table, sine_table, kv_heads, 1.0
    ).astype(jnp.bfloat16)
    values_own = matrix_multiply(normed_low, value_full).astype(jnp.bfloat16)
    current = jnp.concatenate([keys_own, values_own], 1)
    neighbour = current
    earlier = []
    for hop_number in range(reach):
        neighbour = from_behind(neighbour, "blk", 1)
        earlier.insert(0, neighbour)
    keys_all = jnp.concatenate(earlier + [current], 0)
    flat_segments = segments.reshape(-1)
    padded_segments = jnp.concatenate(
        [jnp.full((reach * block_rows,), -1, jnp.int32), flat_segments]
    )
    query_segments = lax.dynamic_slice_in_dim(
        flat_segments, block_index * block_rows, block_rows, 0
    )
    key_segments = lax.dynamic_slice_in_dim(
        padded_segments, block_index * block_rows, (reach + 1) * block_rows, 0
    )
    key_positions = (block_index - reach) * block_rows + jnp.arange(
        (reach + 1) * block_rows, dtype=jnp.int32
    )
    distance = token_positions[:, None] - key_positions[None, :]
    mask_table = (
        (distance >= 0) & (distance < WINDOW) & (query_segments[:, None] == key_segments[None, :])
    )
    attended, logsum = attend(queries, keys_all, mask_table, query_heads, kv_heads)
    attention_sum = lax.psum(
        matrix_multiply(attended, out_full).astype(jnp.bfloat16), "head"
    ).astype(jnp.float32)
    hidden_one = block_float + attention_sum
    normed_two, scale_two = norm_forward(hidden_one, gain_two)
    normed_two_low = normed_two.astype(jnp.bfloat16)
    hidden_rows = lax.dynamic_slice_in_dim(hidden_one, own_offset, local_rows, 0)
    scale_two_rows = lax.dynamic_slice_in_dim(scale_two, own_offset, local_rows, 0)
    grad_output = cotangent[0]
    gate_value = matrix_multiply(normed_two_low, gate_part)
    up_value = matrix_multiply(normed_two_low, up_part)
    sigmoid_gate = jax.nn.sigmoid(gate_value)
    activated = gate_value * sigmoid_gate
    product_low = (activated * up_value).astype(jnp.bfloat16)
    output = hidden_rows + lax.psum_scatter(
        matrix_multiply(product_low, down_part).astype(jnp.bfloat16),
        "head",
        scatter_dimension=0,
        tiled=True,
    ).astype(jnp.float32)
    grad_block = lax.all_gather(grad_output, "head", axis=0, tiled=True)
    grad_product = matmul_nt(grad_block, down_part)
    grad_down = matmul_tn(product_low, grad_block)
    grad_up_value = (grad_product * activated).astype(jnp.bfloat16)
    grad_gate_value = (
        grad_product * up_value * sigmoid_gate * (1.0 + gate_value * (1.0 - sigmoid_gate))
    ).astype(jnp.bfloat16)
    grad_gate = matmul_tn(normed_two_low, grad_gate_value)
    grad_up = matmul_tn(normed_two_low, grad_up_value)
    grad_normed_block = lax.psum(
        (matmul_nt(grad_gate_value, gate_part) + matmul_nt(grad_up_value, up_part)).astype(
            jnp.bfloat16
        ),
        "head",
    ).astype(jnp.float32)
    grad_hidden_block = grad_block.astype(jnp.float32) + norm_backward(
        hidden_one, scale_two, gain_two, grad_normed_block
    )
    grad_normed_rows = lax.dynamic_slice_in_dim(grad_normed_block, own_offset, local_rows, 0)
    grad_hidden_rows = lax.dynamic_slice_in_dim(grad_hidden_block, own_offset, local_rows, 0)
    grad_attention = grad_hidden_block.astype(jnp.bfloat16)
    grad_gain_two = gain_term(hidden_rows, scale_two_rows, grad_normed_rows)
    grad_attended = matmul_nt(grad_attention, out_full).astype(jnp.bfloat16)
    grad_out_weight = matmul_tn(attended, grad_attention)
    grad_queries, grad_keys_all = attend_back(
        queries, keys_all, mask_table, logsum, grad_attended, query_heads, kv_heads
    )
    pieces = grad_keys_all.reshape(reach + 1, block_rows, grad_keys_all.shape[1])
    carried = pieces[0]
    for hop_number in range(reach):
        carried = (
            from_behind(carried.astype(jnp.bfloat16), "blk", -1).astype(carried.dtype)
            + pieces[hop_number + 1]
        )
    grad_key_lin = apply_rotary(
        carried[:, : kv_heads * HEAD_SIZE], cosine_table, sine_table, kv_heads, -1.0
    ).astype(jnp.bfloat16)
    grad_value_lin = carried[:, kv_heads * HEAD_SIZE :].astype(jnp.bfloat16)
    grad_query_lin = apply_rotary(grad_queries, cosine_table, sine_table, query_heads, -1.0).astype(
        jnp.bfloat16
    )
    grad_query_weight = matmul_tn(normed_low, grad_query_lin)
    grad_key_weight = matmul_tn(normed_low, grad_key_lin)
    grad_value_weight = matmul_tn(normed_low, grad_value_lin)
    grad_normed_one = lax.psum_scatter(
        (
            matmul_nt(grad_query_lin, query_full)
            + matmul_nt(grad_key_lin, key_full)
            + matmul_nt(grad_value_lin, value_full)
        ).astype(jnp.bfloat16),
        "head",
        scatter_dimension=0,
        tiled=True,
    ).astype(jnp.float32)
    tokens_rows = tokens[0].astype(jnp.float32)
    scale_one_rows = lax.dynamic_slice_in_dim(scale_one, own_offset, local_rows, 0)
    grad_inputs = grad_hidden_rows + norm_backward(
        tokens_rows, scale_one_rows, gain_one, grad_normed_one
    )
    grad_gain_one = gain_term(tokens_rows, scale_one_rows, grad_normed_one)
    gain_sums = lax.psum((grad_gain_one, grad_gain_two), ("head", "blk"))
    weight_sums = (
        lax.psum_scatter(
            grad_query_weight.astype(jnp.bfloat16), "blk", scatter_dimension=0, tiled=True
        ).astype(jnp.float32),
        lax.psum_scatter(
            grad_key_weight.astype(jnp.bfloat16), "blk", scatter_dimension=0, tiled=True
        ).astype(jnp.float32),
        lax.psum_scatter(
            grad_value_weight.astype(jnp.bfloat16), "blk", scatter_dimension=0, tiled=True
        ).astype(jnp.float32),
        lax.psum_scatter(
            grad_out_weight.astype(jnp.bfloat16), "blk", scatter_dimension=1, tiled=True
        ).astype(jnp.float32),
        lax.psum_scatter(
            grad_gate.astype(jnp.bfloat16), "blk", scatter_dimension=0, tiled=True
        ).astype(jnp.float32),
        lax.psum_scatter(
            grad_up.astype(jnp.bfloat16), "blk", scatter_dimension=0, tiled=True
        ).astype(jnp.float32),
        lax.psum_scatter(
            grad_down.astype(jnp.bfloat16), "blk", scatter_dimension=1, tiled=True
        ).astype(jnp.float32),
    )
    return (
        output.astype(jnp.bfloat16)[None],
        grad_inputs.astype(jnp.bfloat16)[None],
        weight_sums[0],
        weight_sums[1],
        weight_sums[2],
        weight_sums[3],
        weight_sums[4],
        weight_sums[5],
        weight_sums[6],
        gain_sums[0],
        gain_sums[1],
    )


def solution(mesh):
    return jax.shard_map(
        per_device,
        mesh=mesh,
        in_specs=(
            P("blk", "head", None),
            P(),
            P("blk", "head"),
            P("blk", "head"),
            P("blk", "head"),
            P("head", "blk"),
            P("blk", "head"),
            P("blk", "head"),
            P("head", "blk"),
            P(),
            P(),
            P("blk", "head", None),
        ),
        out_specs=(
            P("blk", "head", None),
            P("blk", "head", None),
            P("blk", "head"),
            P("blk", "head"),
            P("blk", "head"),
            P("head", "blk"),
            P("blk", "head"),
            P("blk", "head"),
            P("head", "blk"),
            P(),
            P(),
        ),
        check_vma=False,
    )
```

profile of v0, /device:TPU:0, one launch (start us, length us, event | category | flops | bytes accessed | tf_op | source)
XLA Modules:
  0.0 1249.4 jit_solution(16448471977232205629)
XLA Ops:
  10.2 25.1 %all_gather.29 = bf16[2048,64]{1,0:T(8,128)(2,1)S(1)} all-gather(bf16[64,64]{1,0:T(8,128)(2,1)} %param.19), channel_id=1, replica_groups=mesh['head'=4,'blk'=32] {'blk'}, dimensions={0}, use_global_device_ids=true | all-gather | bytes 270336 | tf_op jit(solution)/shard_map/all_gather | solution.py:178
  35.3 24.1 %all_gather.30 = bf16[2048,64]{1,0:T(8,128)(2,1)S(1)} all-gather(bf16[64,64]{1,0:T(8,128)(2,1)} %param.20), channel_id=1, replica_groups=mesh['head'=4,'blk'=32] {'blk'}, dimensions={0}, use_global_device_ids=true | all-gather | bytes 270336 | tf_op jit(solution)/shard_map/all_gather | solution.py:179
  73.5 15.8 %all-gather.10.cloned.1.call-done = bf16[2048,512]{1,0:T(8,128)(2,1)} async-done(((bf16[64,512]{1,0:T(8,128)(2,1)}), bf16[2048,512]{1,0:T(8,128)(2,1)}) %all-gather.10.cloned.1.call-update) | async-done | bytes 2097168 | tf_op jit(solution)/shard_map/all_gather | solution.py:177
  94.4 45.2 %while.36 = (s32[]{:T(128)}, bf16[512,512]{0,1:T(8,128)(2,1)}, f32[8,512]{1,0:T(8,128)}, bf16[512,512]{1,0:T(8,128)(2,1)}, bf16[1536,128]{1,0:T(8,128)(2,1)S(1)}...) while((s32[]{:T(128)}, bf16[512,512]{0,1:T(8,128)(2,1)}, ...), condition=%wide.region_4.5_spmd.clone, body=%wide.region_1.4_spmd.clone.sunk | while | flops 212368912 | bytes 10478029 | solution.py:107
  147.3 55.2 %all-reduce.5.cloned.1.call-done = bf16[512,2048]{1,0:T(8,128)(2,1)} async-done(((bf16[512,2048]{1,0:T(8,128)(2,1)}), bf16[512,2048]{1,0:T(8,128)(2,1)}) %all-reduce.5.cloned.1.call-update) | async-done | bytes 2097168 | tf_op jit(solution)/shard_map/psum | solution.py:227
  207.3 45.3 %all-gather.14.cloned.1.call-done = bf16[2048,1408]{1,0:T(8,128)(2,1)} async-done(((bf16[64,1408]{1,0:T(8,128)(2,1)}), bf16[2048,1408]{1,0:T(8,128)(2,1)}) %all-gather.14.cloned.1.call-update) | async-done | bytes 5767184 | tf_op jit(solution)/shard_map/all_gather | solution.py:181
  252.6 8.2 fusion.89
  260.9 41.5 %all-gather.16.cloned.1.call-done = bf16[2048,1408]{1,0:T(8,128)(2,1)} async-done(((bf16[64,1408]{1,0:T(8,128)(2,1)}), bf16[2048,1408]{1,0:T(8,128)(2,1)}) %all-gather.16.cloned.1.call-update) | async-done | bytes 5767184 | tf_op jit(solution)/shard_map/all_gather | solution.py:182
  302.3 8.3 fusion.90
  310.6 23.8 %all-gather.22.cloned.1.call-done = bf16[1,512,2048]{2,1,0:T(8,128)(2,1)} async-done(((bf16[1,128,2048]{2,1,0:T(8,128)(2,1)}), bf16[1,512,2048]{2,1,0:T(8,128)(2,1)}) %all-gather.22.cloned.1.call-update) | async-done | bytes 2097168 | tf_op jit(solution)/shard_map/all_gather | solution.py:247
  334.4 50.5 %all-gather.18.cloned.1.call-done = bf16[1408,2048]{0,1:T(8,128)(2,1)} async-done(((bf16[1408,64]{0,1:T(8,128)(2,1)}), bf16[1408,2048]{0,1:T(8,128)(2,1)}) %all-gather.18.cloned.1.call-update) | async-done | bytes 5767184 | tf_op jit(solution)/shard_map/all_gather | solution.py:183
  384.9 10.3 multiply_convert_fusion.2
  406.8 58.1 %all-reduce.7.cloned.1.call-done = bf16[512,2048]{1,0:T(8,128)(2,1)} async-done(((bf16[512,2048]{1,0:T(8,128)(2,1)}), bf16[512,2048]{1,0:T(8,128)(2,1)}) %all-reduce.7.cloned.1.call-update) | async-done | bytes 2097168 | tf_op jit(solution)/shard_map/psum | solution.py:256
  477.2 90.3 %while.37 = (s32[]{:T(128)}, f32[512,512]{0,1:T(8,128)}, f32[1536,128]{0,1:T(8,128)}, bf16[512,512]{1,0:T(8,128)(2,1)}, bf16[1536,128]{1,0:T(8,128)(2,1)S(1)}, /...) while((s32[]{:T(128)}, f32[512,512]{0,1:T(8,128)}, ...), condition=%wide.region_12.13_spmd.clone, body=%wide.region_10.12_spmd.clone.sunk | while | flops 515440128 | bytes 33323508 | solution.py:152
  633.2 34.4 %reduce-scatter.16.cloned.1.call-done = bf16[64,64]{1,0:T(8,128)(2,1)} async-done(((bf16[2048,64]{1,0:T(8,128)(2,1)}), bf16[64,64]{1,0:T(8,128)(2,1)}) %reduce-scatter.16.cloned.1.call-update) | async-done | bytes 8208 | tf_op jit(solution)/shard_map/reduce_scatter | solution.py:312
  668.9 78.4 %reduce-scatter.18.cloned.1.call-done = bf16[64,64]{1,0:T(8,128)(2,1)} async-done(((bf16[2048,64]{1,0:T(8,128)(2,1)}), bf16[64,64]{1,0:T(8,128)(2,1)}) %reduce-scatter.18.cloned.1.call-update) | async-done | bytes 8208 | tf_op jit(solution)/shard_map/reduce_scatter | solution.py:315
  748.7 30.2 %reduce-scatter.10.cloned.1.call-done = bf16[128,2048]{1,0:T(8,128)(2,1)} async-done(((bf16[512,2048]{1,0:T(8,128)(2,1)}), bf16[128,2048]{1,0:T(8,128)(2,1)}) %reduce-scatter.10.cloned.1.call-update) | async-done | bytes 524304 | tf_op jit(solution)/shard_map/reduce_scatter | solution.py:241
  781.6 79.5 %reduce-scatter.14.cloned.1.call-done = bf16[64,512]{1,0:T(8,128)(2,1)} async-done(((bf16[2048,512]{1,0:T(8,128)(2,1)}), bf16[64,512]{1,0:T(8,128)(2,1)}) %reduce-scatter.14.cloned.1.call-update) | async-done | bytes 65552 | tf_op jit(solution)/shard_map/reduce_scatter | solution.py:309
  862.7 80.4 %reduce-scatter.20.cloned.1.call-done = bf16[512,64]{0,1:T(8,128)(2,1)} async-done(((bf16[512,2048]{0,1:T(8,128)(2,1)}), bf16[512,64]{0,1:T(8,128)(2,1)}) %reduce-scatter.20.cloned.1.call-update) | async-done | bytes 65552 | tf_op jit(solution)/shard_map/reduce_scatter | solution.py:318
  944.6 30.3 %reduce-scatter.12.cloned.1.call-done = bf16[128,2048]{1,0:T(8,128)(2,1)} async-done(((bf16[512,2048]{1,0:T(8,128)(2,1)}), bf16[128,2048]{1,0:T(8,128)(2,1)}) %reduce-scatter.12.cloned.1.call-update) | async-done | bytes 524304 | tf_op jit(solution)/shard_map/reduce_scatter | solution.py:291
  976.3 65.8 %all-reduce.1 = (f32[2048]{0:T(1024)}, f32[2048]{0:T(1024)}) all-reduce(f32[2048]{0:T(1024)S(1)} %get-tuple-element.463, f32[2048]{0:T(1024)S(1)} %get-tuple-element.514), channel_id=1, replica_groups=mesh['head'=4,'blk'=32] {'head','blk'}, use_global_device_ids=true, to_apply=%region_23.24 | all-reduce | flops 4096 | bytes 32768 | tf_op jit(solution)/shard_map/psum | solution.py:307
  1044.6 19.1 %reduce-scatter.22.cloned.1.call-done = bf16[64,1408]{1,0:T(8,128)(2,1)} async-done(((bf16[2048,1408]{1,0:T(8,128)(2,1)}), bf16[64,1408]{1,0:T(8,128)(2,1)}) %reduce-scatter.22.cloned.1.call-update) | async-done | bytes 180240 | tf_op jit(solution)/shard_map/reduce_scatter | solution.py:321
  1065.4 87.0 %reduce-scatter.24.cloned.1.call-done = bf16[64,1408]{1,0:T(8,128)(2,1)} async-done(((bf16[2048,1408]{1,0:T(8,128)(2,1)}), bf16[64,1408]{1,0:T(8,128)(2,1)}) %reduce-scatter.24.cloned.1.call-update) | async-done | bytes 180240 | tf_op jit(solution)/shard_map/reduce_scatter | solution.py:324
  1154.1 86.5 %reduce-scatter.26.cloned.1.call-done = bf16[1408,64]{0,1:T(8,128)(2,1)} async-done(((bf16[1408,2048]{0,1:T(8,128)(2,1)}), bf16[1408,64]{0,1:T(8,128)(2,1)}) %reduce-scatter.26.cloned.1.call-update) | async-done | bytes 180240 | tf_op jit(solution)/shard_map/reduce_scatter | solution.py:327
  (354 shorter events, 275.8 us)
Async XLA Ops:
  7.2 52.3 %all-gather.20.cloned.1.call-start = ((), (), s32[]{:S(2)}) async-start(), calls=%async_computation.25 | async-start | bytes 2621440 | tf_op jit(solution)/shard_map/all_gather | solution.py:189
  7.9 81.4 %all-gather.10.cloned.1.call-start = ((), (), s32[]{:S(2)}) async-start(), calls=%async_computation.9 | async-start | bytes 2162688 | tf_op jit(solution)/shard_map/all_gather | solution.py:177
  8.7 130.9 %all-gather.12.cloned.1.call-start = ((), (), s32[]{:S(2)}) async-start(), calls=%async_computation.10 | async-start | bytes 2162688 | tf_op jit(solution)/shard_map/all_gather | solution.py:180
  9.4 193.1 %all-reduce.5.cloned.1.call-start = ((), (), s32[]{:S(2)}) async-start(), calls=%async_computation.11 | async-start | bytes 4194304 | tf_op jit(solution)/shard_map/psum | solution.py:227
  65.5 3.2 collective-permute-start
  68.7 4.6 collective-permute-start.1
  144.0 108.7 %all-gather.14.cloned.1.call-start = ((), (), s32[]{:S(2)}) async-start(), calls=%async_computation.12 | async-start | bytes 5947392 | tf_op jit(solution)/shard_map/all_gather | solution.py:181
  144.6 157.8 %all-gather.16.cloned.1.call-start = ((), (), s32[]{:S(2)}) async-start(), calls=%async_computation.13 | async-start | bytes 5947392 | tf_op jit(solution)/shard_map/all_gather | solution.py:182
  145.2 189.2 %all-gather.22.cloned.1.call-start = ((), (), s32[]{:S(2)}) async-start(), calls=%async_computation.26 | async-start | bytes 2621440 | tf_op jit(solution)/shard_map/all_gather | solution.py:247
  145.9 239.0 %all-gather.18.cloned.1.call-start = ((), (), s32[]{:S(2)}) async-start(), calls=%async_computation.14 | async-start | bytes 5947392 | tf_op jit(solution)/shard_map/all_gather | solution.py:183
  146.7 318.3 %all-reduce.7.cloned.1.call-start = ((), (), s32[]{:S(2)}) async-start(), calls=%async_computation.16 | async-start | bytes 4194304 | tf_op jit(solution)/shard_map/psum | solution.py:256
  406.6 261.0 %reduce-scatter.16.cloned.1.call-start = ((), (), s32[]{:S(2)}) async-start(), calls=%async_computation.19 | async-start | bytes 540672 | tf_op jit(solution)/shard_map/reduce_scatter | solution.py:312
  477.2 103.2 %copy-start.28 = (f32[2048]{0:T(1024)S(1)}, f32[2048]{0:T(1024)}, u32[]{:S(2)}) copy-start(f32[2048]{0:T(1024)} %copy-done.27) | copy-start | bytes 24580
  568.4 3.2 collective-permute-start.2
  572.6 5.8 collective-permute-start.3
  583.8 163.5 %reduce-scatter.18.cloned.1.call-start = ((), (), s32[]{:S(2)}) async-start(), calls=%async_computation.20 | async-start | bytes 540672 | tf_op jit(solution)/shard_map/reduce_scatter | solution.py:315
  585.8 193.2 %reduce-scatter.10.cloned.1.call-start = ((), (), s32[]{:S(2)}) async-start(), calls=%async_computation.15 | async-start | bytes 2621440 | tf_op jit(solution)/shard_map/reduce_scatter | solution.py:241
  593.8 267.4 %reduce-scatter.14.cloned.1.call-start = ((), (), s32[]{:S(2)}) async-start(), calls=%async_computation.18 | async-start | bytes 2162688 | tf_op jit(solution)/shard_map/reduce_scatter | solution.py:309
  597.3 345.8 %reduce-scatter.20.cloned.1.call-start = ((), (), s32[]{:S(2)}) async-start(), calls=%async_computation.21 | async-start | bytes 2162688 | tf_op jit(solution)/shard_map/reduce_scatter | solution.py:318
  602.2 372.7 %reduce-scatter.12.cloned.1.call-start = ((), (), s32[]{:S(2)}) async-start(), calls=%async_computation.17 | async-start | bytes 2621440 | tf_op jit(solution)/shard_map/reduce_scatter | solution.py:291
  608.4 455.3 %reduce-scatter.22.cloned.1.call-start = ((), (), s32[]{:S(2)}) async-start(), calls=%async_computation.22 | async-start | bytes 5947392 | tf_op jit(solution)/shard_map/reduce_scatter | solution.py:321
  615.1 537.3 %reduce-scatter.24.cloned.1.call-start = ((), (), s32[]{:S(2)}) async-start(), calls=%async_computation.23 | async-start | bytes 5947392 | tf_op jit(solution)/shard_map/reduce_scatter | solution.py:324
  621.7 618.9 %reduce-scatter.26.cloned.1.call-start = ((), (), s32[]{:S(2)}) async-start(), calls=%async_computation.24 | async-start | bytes 5947392 | tf_op jit(solution)/shard_map/reduce_scatter | solution.py:327
  633.2 341.7 %copy-start.10 = (bf16[1,128,2048]{2,1,0:T(8,128)(2,1)S(1)}, bf16[1,128,2048]{2,1,0:T(8,128)(2,1)}, u32[]{:S(2)}) copy-start(bf16[1,128,2048]{2,1,0:T(8,128)(2,1)} %param.16) | copy-start | bytes 1572868
  (70 other events, 443.5 us)
Sparse Core Ops, SparseCore 0:
  9.7 33.5 all-gather.19
  45.5 43.8 all-gather.9
  91.6 43.0 all-gather.11
  144.1 58.3 all-reduce.4
  204.8 47.7 all-gather.13
  255.0 47.2 all-gather.15
  304.1 30.2 all-gather.21
  336.9 47.9 all-gather.17
  406.7 58.1 all-reduce.6
  584.0 83.5 reduce-scatter.15
  671.0 76.2 reduce-scatter.17
  749.6 29.2 reduce-scatter.9
  782.9 78.2 reduce-scatter.13
  865.0 78.0 reduce-scatter.19
  945.5 29.3 reduce-scatter.11
  978.5 85.2 reduce-scatter.21
  1067.8 84.5 reduce-scatter.23
  1156.0 84.5 reduce-scatter.25
where the time goes:
time: 1260 us; the launch traced here: 1250 us
  waiting for transfers between devices  827 us (66%)
  matrix products  192 us (15%)
  blocking collectives  115 us (9%)
  other arithmetic  47.7 us (4%)
  local copies, waits for them, and re-layouts  41.8 us (3%)
  between operations  15.1 us (1%)
    reduce_scatter x1, waiting for transfers between devices, per_device(): lax.psum_scatter(grad_up.astype(jnp.bfloat16), 'blk', scatter_dimension=0...  87 us
    reduce_scatter x1, waiting for transfers between devices, per_device(): lax.psum_scatter(grad_down.astype(jnp.bfloat16), 'blk', scatter_dimension...  86.5 us
    dot_general x31, matrix products, matmul_nt(): lax.dot_general(former, latter, (((1,), (1,)), ((), ())), preferred_eleme...  80.8 us
    reduce_scatter x1, waiting for transfers between devices, per_device(): lax.psum_scatter(grad_out_weight.astype(jnp.bfloat16), 'blk', scatter_dim...  80.4 us
    reduce_scatter x1, waiting for transfers between devices, per_device(): lax.psum_scatter(grad_query_weight.astype(jnp.bfloat16), 'blk', scatter_d...  79.5 us
    reduce_scatter x1, waiting for transfers between devices, per_device(): lax.psum_scatter(grad_value_weight.astype(jnp.bfloat16), 'blk', scatter_d...  78.4 us
    psum x1, blocking collectives, per_device(): gain_sums = lax.psum((grad_gain_one, grad_gain_two), ('head', 'blk'))  65.8 us
    dot_general x23, matrix products, matrix_multiply(): return jnp.dot(former, latter, preferred_element_type=jnp.float32)  58.8 us
  transfers between devices with their start and end apart: 22, of which 18 were waited for; matrix products, arithmetic and copies ran while one was open for 11% of the time, Pallas kernels for 0%

commit v1 on v0

v1 whole, which is shorter than its diff:
```python
import functools

import jax
import jax.numpy as jnp
from jax import lax
from jax.experimental import pallas as pl
from jax.experimental.pallas import tpu as pltpu
from jax.sharding import Mesh
from jax.sharding import PartitionSpec as P

HEAD_SIZE = 64
WINDOW = 1024
EPSILON = 1e-05
BF16 = jnp.bfloat16
F32 = jnp.float32
BLK = ("y", "x", "core")
VMEM_LIMIT = 56 * 1024 * 1024


def dot_nn(a, b):
    return jnp.dot(a, b, preferred_element_type=F32)


def dot_nt(a, b):
    return lax.dot_general(a, b, (((1,), (1,)), ((), ())), preferred_element_type=F32)


def dot_tn(a, b):
    return lax.dot_general(a, b, (((0,), (0,)), ((), ())), preferred_element_type=F32)


def shift(value, axis, distance):
    size = lax.axis_size(axis)
    return lax.ppermute(value, axis, [(i, (i + distance) % size) for i in range(size)])


def add_low(a, b):
    return (a.astype(F32) + b.astype(F32)).astype(BF16)


def gather_head(rows):
    half = rows.shape[0] // 2
    top, bottom = rows[:half], rows[half:]
    behind_top = shift(top, "head", 1)
    ahead_bottom = shift(bottom, "head", -1)
    behind_bottom = shift(bottom, "head", 1)
    ahead_top = shift(top, "head", -1)
    far_top = shift(behind_top, "head", 1)
    far_bottom = shift(ahead_bottom, "head", -1)
    return jnp.concatenate(
        [rows, ahead_top, ahead_bottom, far_top, far_bottom, behind_top, behind_bottom], 0
    )


def scatter_head(partial):
    n = partial.shape[0] // 4
    half = n // 2
    own, ahead, far, behind = (partial[k * n : (k + 1) * n] for k in range(4))
    far_top = shift(far[:half], "head", 1)
    far_bottom = shift(far[half:], "head", -1)
    from_behind_bottom = shift(ahead[half:], "head", 1)
    from_ahead_top = shift(behind[:half], "head", -1)
    from_behind_top = shift(add_low(ahead[:half], far_top), "head", 1)
    from_ahead_bottom = shift(add_low(behind[half:], far_bottom), "head", -1)
    own = own.astype(F32)
    top = own[:half] + from_behind_top.astype(F32) + from_ahead_top.astype(F32)
    bottom = own[half:] + from_behind_bottom.astype(F32) + from_ahead_bottom.astype(F32)
    return jnp.concatenate([top, bottom], 0)


def scatter_axis(value, axis, dim):
    index = lax.axis_index(axis)

    def pick(distance):
        return lax.dynamic_index_in_dim(value, (index + distance) % 4, dim, False)

    ahead, behind, far = (
        shift(pick(1), axis, 1),
        shift(pick(3), axis, -1),
        shift(pick(2), axis, 2),
    )
    return pick(0).astype(F32) + ahead.astype(F32) + behind.astype(F32) + far.astype(F32)


def scatter_blocks(value):
    rows = value.shape[0] // 32
    half = rows // 2
    core = lax.axis_index("core")
    shaped = value.reshape(16, 2, rows, value.shape[1])
    other = shift(lax.dynamic_index_in_dim(shaped, 1 - core, 1, False), "core", 1)
    pair = add_low(lax.dynamic_index_in_dim(shaped, core, 1, False), other)
    pair = pair.reshape(4, 4, rows, value.shape[1])
    first = scatter_axis(pair[:, :, :half], "x", 1).astype(BF16)
    second = scatter_axis(pair[:, :, half:], "y", 0).astype(BF16)
    first = scatter_axis(first, "y", 0)
    second = scatter_axis(second, "x", 0)
    return jnp.concatenate([first, second], 0)


def sum_everywhere(value):
    for axis in ("head", "y", "x"):
        value = (value + shift(value, axis, 1)) + (shift(value, axis, -1) + shift(value, axis, 2))
    return value + shift(value, "core", 1)


def from_block(value, distance):
    route = [(i, i + distance) for i in range(32) if 0 <= i + distance < 32]
    return lax.ppermute(value, BLK, route)


def scale_of(values):
    return lax.rsqrt(jnp.mean(values * values, -1, keepdims=True) + EPSILON)


def norm_backward(values, scale, gain, grad):
    weighted = grad * gain
    inner = jnp.mean(weighted * values, -1, keepdims=True)
    return scale * weighted - values * (scale * scale * scale * inner)


def lane_is_low(shape, period):
    return lax.broadcasted_iota(jnp.int32, shape, len(shape) - 1) % period < period // 2


def turn(values, cosine, sine):
    swapped = jnp.where(
        lane_is_low(values.shape, 64), pltpu.roll(values, 96, 1), pltpu.roll(values, 32, 1)
    )
    return values * cosine + swapped * sine


def project_kernel(x_ref, w_ref, cos_ref, sin_ref, q_ref, kv_ref):
    cosine, sine = cos_ref[...], sin_ref[...]
    x = x_ref[...]
    for start in (0, 256):
        wide = dot_nn(x, w_ref[:, start : start + 256])
        for part in (0, 128):
            turned = turn(wide[:, part : part + 128], cosine, sine)
            q_ref[:, start + part : start + part + 128] = (turned * HEAD_SIZE**-0.5).astype(BF16)
    last = dot_nn(x, w_ref[:, 512:640])
    kv_ref[...] = jnp.where(lane_is_low(last.shape, 128), turn(last, cosine, sine), last).astype(BF16)


def project(normed, weights, cosine, sine):
    rows, width = normed.shape
    return pl.pallas_call(
        project_kernel,
        out_shape=(
            jax.ShapeDtypeStruct((rows, 512), BF16),
            jax.ShapeDtypeStruct((rows, 128), BF16),
        ),
        grid=(1,),
        in_specs=[
            pl.BlockSpec((rows, width), lambda i: (0, 0)),
            pl.BlockSpec((width, 640), lambda i: (0, 0)),
            pl.BlockSpec((rows, 128), lambda i: (0, 0)),
            pl.BlockSpec((rows, 128), lambda i: (0, 0)),
        ],
        out_specs=(
            pl.BlockSpec((rows, 512), lambda i: (0, 0)),
            pl.BlockSpec((rows, 128), lambda i: (0, 0)),
        ),
        compiler_params=pltpu.CompilerParams(vmem_limit_bytes=VMEM_LIMIT),
        cost_estimate=pl.CostEstimate(
            flops=2 * rows * width * 640, bytes_accessed=6 * 1024 * 1024, transcendentals=0
        ),
    )(normed, weights, cosine, sine)


def set_up(place, kv0_ref, kv1_ref, kv2_ref, qseg_ref, kseg_ref, kk, vv, kvt, bias):
    low = lane_is_low((128, 128), 128)
    for block, ref in enumerate((kv0_ref, kv1_ref, kv2_ref)):
        for group in range(4):
            at = pl.multiple_of(lax.rem(group - place + 4, 4) * 128, 128)
            piece = ref[pl.ds(at, 128), :].astype(F32)
            rolled = pltpu.roll(piece, 64, 1)
            to = block * 512 + group * 128
            kk[to : to + 128, :] = jnp.where(low, piece, rolled).astype(BF16)
            vv[to : to + 128, :] = jnp.where(low, rolled, piece).astype(BF16)
            kvt[:, to : to + 128] = piece.T.astype(BF16)
    for tile in range(2):
        key = lax.broadcasted_iota(jnp.int32, (1280, 256), 0)
        query = lax.broadcasted_iota(jnp.int32, (1280, 256), 1)
        distance = query - key + WINDOW
        same = kseg_ref[256 * tile : 256 * tile + 1280, :] == qseg_ref[:, 256 * tile : 256 * tile + 256]
        seen = (distance >= 0) & (distance < WINDOW) & same
        bias[tile] = jnp.where(seen, 0.0, -jnp.inf)


def true_rows(ref, place, tile):
    pieces = []
    for group in (0, 1):
        at = pl.multiple_of(lax.rem(2 * tile + group - place + 4, 4) * 128, 128)
        pieces.append(ref[pl.ds(at, 128), :])
    return jnp.concatenate(pieces, 0)


def put_rows(ref, place, tile, value):
    for group in (0, 1):
        at = pl.multiple_of(lax.rem(2 * tile + group - place + 4, 4) * 128, 128)
        ref[pl.ds(at, 128), :] = value[128 * group : 128 * group + 128]


def attend_kernel(
    place_ref, q_ref, kv0_ref, kv1_ref, kv2_ref, qseg_ref, kseg_ref, o_ref, lse_ref, kk, vv, kvt, bias
):
    place = place_ref[0]

    @pl.when(pl.program_id(0) == 0)
    def _():
        set_up(place, kv0_ref, kv1_ref, kv2_ref, qseg_ref, kseg_ref, kk, vv, kvt, bias)

    low = lane_is_low((256, 128), 128)
    for tile in range(2):
        keys = slice(256 * tile, 256 * tile + 1280)
        pair = true_rows(q_ref, place, tile)
        results = []
        for head in range(2):
            query = jnp.where(low if head == 0 else ~low, pair, jnp.zeros_like(pair))
            scores = dot_nt(kk[keys, :], query) + bias[tile]
            top = jnp.max(scores, 0, keepdims=True)
            weights = jnp.exp(scores - top)
            total = jnp.sum(weights, 0, keepdims=True)
            results.append(dot_nn(kvt[64:128, keys], weights.astype(BF16)) / total)
            lse_ref[0, head : head + 1, 256 * tile : 256 * tile + 256] = top + jnp.log(total)
        put_rows(o_ref, place, tile, jnp.concatenate(results, 0).T.astype(BF16))


ATTENTION_SCRATCH = [
    pltpu.VMEM((1536, 128), BF16),
    pltpu.VMEM((1536, 128), BF16),
    pltpu.VMEM((128, 1536), BF16),
    pltpu.VMEM((2, 1280, 256), F32),
]


def attend(place, queries, kv, qseg, kseg):
    whole = lambda p, s: (0, 0)
    grid = pltpu.PrefetchScalarGridSpec(
        num_scalar_prefetch=1,
        grid=(4,),
        in_specs=[
            pl.BlockSpec((512, 128), lambda p, s: (0, p)),
            pl.BlockSpec((512, 128), whole),
            pl.BlockSpec((512, 128), whole),
            pl.BlockSpec((512, 128), whole),
            pl.BlockSpec((1, 512), whole),
            pl.BlockSpec((1536, 1), whole),
        ],
        out_specs=(
            pl.BlockSpec((512, 128), lambda p, s: (0, p)),
            pl.BlockSpec((1, 2, 512), lambda p, s: (p, 0, 0)),
        ),
        scratch_shapes=ATTENTION_SCRATCH,
    )
    return pl.pallas_call(
        attend_kernel,
        grid_spec=grid,
        out_shape=(
            jax.ShapeDtypeStruct((512, 512), BF16),
            jax.ShapeDtypeStruct((4, 2, 512), F32),
        ),
        compiler_params=pltpu.CompilerParams(vmem_limit_bytes=VMEM_LIMIT),
        cost_estimate=pl.CostEstimate(
            flops=8 * 512 * 1280 * 256 * 2, bytes_accessed=4 * 1024 * 1024, transcendentals=8 * 512 * 1280
        ),
    )(place, queries, *kv, qseg, kseg)


def attend_back_kernel(
    place_ref,
    q_ref,
    do_ref,
    lse_ref,
    kv0_ref,
    kv1_ref,
    kv2_ref,
    qseg_ref,
    kseg_ref,
    cos_ref,
    sin_ref,
    dq_ref,
    dkv_ref,
    kk,
    vv,
    kvt,
    bias,
    dk,
    dv,
):
    place = place_ref[0]

    @pl.when(pl.program_id(0) == 0)
    def _():
        set_up(place, kv0_ref, kv1_ref, kv2_ref, qseg_ref, kseg_ref, kk, vv, kvt, bias)
        dk[...] = jnp.zeros_like(dk)
        dv[...] = jnp.zeros_like(dv)

    low = lane_is_low((256, 128), 128)
    for tile in range(2):
        keys = slice(256 * tile, 256 * tile + 1280)
        pair = true_rows(q_ref, place, tile)
        grad_pair = true_rows(do_ref, place, tile)
        results = []
        for head in range(2):
            mask = low if head == 0 else ~low
            query = jnp.where(mask, pair, jnp.zeros_like(pair))
            grad = jnp.where(mask, grad_pair, jnp.zeros_like(pair))
            scores = dot_nt(kk[keys, :], query) + bias[tile]
            weights = jnp.exp(scores - lse_ref[0, head : head + 1, 256 * tile : 256 * tile + 256])
            grad_weights = dot_nt(vv[keys, :], grad)
            dv[keys, :] += dot_nn(weights.astype(BF16), grad)
            inner = jnp.sum(weights * grad_weights, 0, keepdims=True)
            grad_scores = (weights * (grad_weights - inner)).astype(BF16)
            dk[keys, :] += dot_nn(grad_scores, query)
            results.append(dot_nn(kvt[0:64, keys], grad_scores))
        grad_query = jnp.concatenate(results, 0).T * HEAD_SIZE**-0.5
        turned = turn(
            grad_query, true_rows(cos_ref, place, tile), -true_rows(sin_ref, place, tile)
        )
        put_rows(dq_ref, place, tile, turned.astype(BF16))

    @pl.when(pl.program_id(0) == 3)
    def _():
        half = lane_is_low((128, 128), 128)
        for block in range(3):
            for group in range(4):
                at = pl.multiple_of(lax.rem(group - place + 4, 4) * 128, 128)
                frm = slice(block * 512 + group * 128, block * 512 + group * 128 + 128)
                key, value = dk[frm, :], dv[frm, :]
                key = key + pltpu.roll(key, 64, 1)
                value = value + pltpu.roll(value, 64, 1)
                dkv_ref[block, pl.ds(at, 128), :] = jnp.where(half, key, value)


def attend_back(place, queries, grad_attended, lse, kv, qseg, kseg, cosine, sine):
    whole = lambda p, s: (0, 0)
    grid = pltpu.PrefetchScalarGridSpec(
        num_scalar_prefetch=1,
        grid=(4,),
        in_specs=[
            pl.BlockSpec((512, 128), lambda p, s: (0, p)),
            pl.BlockSpec((512, 128), lambda p, s: (0, p)),
            pl.BlockSpec((1, 2, 512), lambda p, s: (p, 0, 0)),
            pl.BlockSpec((512, 128), whole),
            pl.BlockSpec((512, 128), whole),
            pl.BlockSpec((512, 128), whole),
            pl.BlockSpec((1, 512), whole),
            pl.BlockSpec((1536, 1), whole),
            pl.BlockSpec((512, 128), whole),
            pl.BlockSpec((512, 128), whole),
        ],
        out_specs=(
            pl.BlockSpec((512, 128), lambda p, s: (0, p)),
            pl.BlockSpec((3, 512, 128), lambda p, s: (0, 0, 0)),
        ),
        scratch_shapes=ATTENTION_SCRATCH
        + [pltpu.VMEM((1536, 128), F32), pltpu.VMEM((1536, 128), F32)],
    )
    return pl.pallas_call(
        attend_back_kernel,
        grid_spec=grid,
        out_shape=(
            jax.ShapeDtypeStruct((512, 512), BF16),
            jax.ShapeDtypeStruct((3, 512, 128), F32),
        ),
        compiler_params=pltpu.CompilerParams(vmem_limit_bytes=VMEM_LIMIT),
        cost_estimate=pl.CostEstimate(
            flops=8 * 512 * 1280 * 640 * 2, bytes_accessed=6 * 1024 * 1024, transcendentals=8 * 512 * 1280
        ),
    )(place, queries, grad_attended, lse, *kv, qseg, kseg, cosine, sine)


def weight_grad_kernel(normed_ref, dy_ref, dgu_ref, act_ref, out_ref):
    part = pl.program_id(0)

    @pl.when(part < 2)
    def _():
        out_ref[...] = dot_tn(normed_ref[...], dgu_ref[...]).astype(BF16)

    @pl.when(part == 2)
    def _():
        out_ref[...] = dot_tn(dy_ref[...], act_ref[...]).astype(BF16)


def weight_grads(normed, dy, dgu, act):
    rows, width = normed.shape
    hidden = act.shape[1]
    tile = 256
    return pl.pallas_call(
        weight_grad_kernel,
        out_shape=jax.ShapeDtypeStruct((width, 3 * hidden), BF16),
        grid=(3, width // tile),
        in_specs=[
            pl.BlockSpec((rows, tile), lambda j, i: (0, i)),
            pl.BlockSpec((rows, tile), lambda j, i: (0, i)),
            pl.BlockSpec((rows, hidden), lambda j, i: (0, jnp.minimum(j, 1))),
            pl.BlockSpec((rows, hidden), lambda j, i: (0, 0)),
        ],
        out_specs=pl.BlockSpec((tile, hidden), lambda j, i: (i, j)),
        compiler_params=pltpu.CompilerParams(vmem_limit_bytes=VMEM_LIMIT),
        cost_estimate=pl.CostEstimate(
            flops=2 * 3 * rows * width * hidden, bytes_accessed=30 * 1024 * 1024, transcendentals=0
        ),
    )(normed, dy, dgu, act)


def per_device(
    tokens,
    segments,
    w_query,
    key_projection,
    value_projection,
    w_out,
    w_gate,
    w_up,
    w_down,
    norm_attn,
    norm_ffn,
    cotangent,
):
    place = lax.axis_index("head")
    block = (lax.axis_index("y") * 4 + lax.axis_index("x")) * 2 + lax.axis_index("core")
    place_array = place.astype(jnp.int32).reshape(1)

    attention_weights = lax.all_gather(
        jnp.concatenate([w_query, key_projection, value_projection, w_out.T], 1), BLK, axis=0, tiled=True
    )
    ffn_weights = lax.all_gather(
        jnp.concatenate([w_gate, w_up, w_down.T], 1), BLK, axis=0, tiled=True
    )
    out_t = attention_weights[:, 640:]

    gain_one, gain_two = norm_attn.astype(F32), norm_ffn.astype(F32)
    x_rows = tokens[0].astype(F32)
    scale_one = scale_of(x_rows)
    normed_one = gather_head((x_rows * scale_one * gain_one).astype(BF16))

    row = jnp.arange(512, dtype=jnp.int32)
    positions = block * 512 + ((row // 128 + place) % 4) * 128 + row % 128
    frequency = 10000.0 ** (-jnp.arange(32, dtype=F32) * 2.0 / HEAD_SIZE)
    angles = positions.astype(F32)[:, None] * frequency[None, :]
    cosine, sine = jnp.cos(angles), jnp.sin(angles)
    cosine = jnp.concatenate([cosine] * 4, 1)
    sine = jnp.concatenate([-sine, sine, -sine, sine], 1)

    queries, kv_own = project(normed_one, attention_weights, cosine, sine)
    kv = (from_block(kv_own, 2), from_block(kv_own, 1), kv_own)

    flat = segments.reshape(-1)
    padded = jnp.concatenate([jnp.full((1024,), -1, jnp.int32), flat])
    qseg = lax.dynamic_slice_in_dim(flat, block * 512, 512, 0).reshape(1, 512)
    kseg = lax.dynamic_slice_in_dim(padded, block * 512, 1536, 0).reshape(1536, 1)

    attended, lse = attend(place_array, queries, kv, qseg, kseg)
    h1 = x_rows + scatter_head(dot_nt(attended, out_t).astype(BF16))
    scale_two = scale_of(h1)
    normed_two = gather_head((h1 * scale_two * gain_two).astype(BF16))

    dy = gather_head(cotangent[0])
    gate = dot_nn(normed_two, ffn_weights[:, :1408])
    up = dot_nn(normed_two, ffn_weights[:, 1408:2816])
    dact = dot_nn(dy, ffn_weights[:, 2816:])
    sig = jax.nn.sigmoid(gate)
    silu = gate * sig
    act = (silu * up).astype(BF16)
    dgate = (dact * up * (sig * (1.0 + gate * (1.0 - sig)))).astype(BF16)
    dup = (dact * silu).astype(BF16)
    dgu = jnp.concatenate([dgate, dup], 1)
    output = h1 + scatter_head(dot_nt(act, ffn_weights[:, 2816:]).astype(BF16))
    dnormed_two = scatter_head(dot_nt(dgu, ffn_weights[:, :2816]).astype(BF16))

    ffn_grads = lax.psum_scatter(
        weight_grads(normed_two, dy, dgu, act), BLK, scatter_dimension=0, tiled=True
    )

    dh1 = cotangent[0].astype(F32) + norm_backward(h1, scale_two, gain_two, dnormed_two)
    grad_gain_two = jnp.sum(dnormed_two * h1 * scale_two, 0)
    dh1_low = gather_head(dh1.astype(BF16))
    dattended = dot_nn(dh1_low, out_t).astype(BF16)
    grad_out_t = dot_tn(dh1_low, attended).astype(BF16)

    dq, dkv = attend_back(place_array, queries, dattended, lse, kv, qseg, kseg, cosine, sine)
    dkv_own = (
        dkv[2]
        + from_block(dkv[1].astype(BF16), -1).astype(F32)
        + from_block(dkv[0].astype(BF16), -2).astype(F32)
    )
    dk_own = dkv_own[:, :64]
    swapped = jnp.concatenate([dk_own[:, 32:], dk_own[:, :32]], 1)
    dk_own = dk_own * cosine[:, :64] - swapped * sine[:, :64]
    dqkv = jnp.concatenate([dq, dk_own.astype(BF16), dkv_own[:, 64:].astype(BF16)], 1)

    qkv_weights = attention_weights[:, :640]
    dnormed_one = scatter_head(dot_nt(dqkv, qkv_weights).astype(BF16))
    grad_inputs = dh1 + norm_backward(x_rows, scale_one, gain_one, dnormed_one)
    grad_qkv = dot_tn(normed_one, dqkv)
    grad_gain_one = jnp.sum(grad_qkv * qkv_weights.astype(F32), 1) / gain_one
    gains = sum_everywhere(jnp.stack([grad_gain_one, grad_gain_two]))
    attention_grads = scatter_blocks(jnp.concatenate([grad_qkv.astype(BF16), grad_out_t], 1))

    return (
        output.astype(BF16)[None],
        grad_inputs.astype(BF16)[None],
        attention_grads[:, :512],
        attention_grads[:, 512:576],
        attention_grads[:, 576:640],
        attention_grads[:, 640:].T,
        ffn_grads[:, :1408].astype(F32),
        ffn_grads[:, 1408:2816].astype(F32),
        ffn_grads[:, 2816:].T.astype(F32),
        gains[0],
        gains[1],
    )


def solution(mesh):
    grid = Mesh(mesh.devices.reshape(4, 4, 4, 2), ("head", "y", "x", "core"))
    rows, up, down = P(BLK, "head", None), P(BLK, "head"), P("head", BLK)
    return jax.shard_map(
        per_device,
        mesh=grid,
        in_specs=(rows, P(), up, up, up, down, up, up, down, P(), P(), rows),
        out_specs=(rows, rows, up, up, up, down, up, up, down, P(), P()),
        check_vma=False,
    )
```

time: 1260 us -> 435 us (0.35)
  waiting for transfers between devices: 827 us -> 98.2 us
  matrix products: 192 us -> 55.9 us
  blocking collectives: 115 us -> 0 us
  starting transfers between devices: 10 us -> 114 us
  Pallas kernels: 0 us -> 71.6 us
  other arithmetic: 47.7 us -> 29 us
    reduce_scatter x9 -> x1, waiting for transfers between devices: 526 us -> 0.01 us  [per_device(): lax.psum_scatter(weight_grads(normed_two, dy, dgu, act), BLK, scatter_dim...]
    all_gather x7 -> x2, waiting for transfers between devices: 177 us -> 3.16 us  [the longest x1 3.15 us: per_device(): lax.all_gather(jnp.concatenate([w_query, key_projection, value_projection...]
    dot_general x77 -> x10, matrix products: 192 us -> 55.9 us  [the longest x4 25.4 us: dot_nn(): return jnp.dot(a, b, preferred_element_type=F32)]
    psum x2 -> x0, waiting for transfers between devices: 113 us -> none  [the longest x1 58.1 us: per_device(): lax.psum((matmul_nt(grad_gate_value, gate_part) + matmul_nt(grad_up_value...]
    ppermute x4 -> x75, starting transfers between devices: 8.12 us -> 114 us  [the longest x71 106 us: shift(): lax.ppermute(value, axis, [(i, (i + distance) % size) for i in range(size)])]
    ppermute x4 -> x75, waiting for transfers between devices: 6.29 us -> 95 us  [the longest x71 80.5 us: shift(): lax.ppermute(value, axis, [(i, (i + distance) % size) for i in range(size)])]
    pallas_call x0 -> x4, Pallas kernels: none -> 71.6 us  [the longest x1 26.3 us: weight_grads(): pl.pallas_call(weight_grad_kernel, out_shape=jax.ShapeDtypeStruct((width,...]
    psum x1 -> x0, blocking collectives: 65.8 us -> none  [per_device(): gain_sums = lax.psum((grad_gain_one, grad_gain_two), ('head', 'blk'))]
  transfers between devices with their start and end apart: 22 -> 78, of which waited for: 18 -> 33; matrix products, arithmetic and copies ran while one was open for 11% -> 23% of each run, Pallas kernels for 0% -> 11%
where the time goes in v1:
time: 435 us; the launch traced here: 427 us
  starting transfers between devices  114 us (26%)
  waiting for transfers between devices  98.2 us (23%)
  Pallas kernels  71.6 us (16%)
  matrix products  55.9 us (13%)
  local copies, waits for them, and re-layouts  42.9 us (10%)
  other arithmetic  29 us (7%)
  between operations  15.3 us (4%)
    ppermute x71, starting transfers between devices, shift(): lax.ppermute(value, axis, [(i, (i + distance) % size) for i in range(size)])  106 us
    ppermute x71, waiting for transfers between devices, shift(): lax.ppermute(value, axis, [(i, (i + distance) % size) for i in range(size)])  80.5 us
    pallas_call x1, Pallas kernels, weight_grads(): pl.pallas_call(weight_grad_kernel, out_shape=jax.ShapeDtypeStruct((width,...  26.3 us
    dot_general x4, matrix products, dot_nn(): return jnp.dot(a, b, preferred_element_type=F32)  25.4 us
    dot_general x4, matrix products, dot_nt(): lax.dot_general(a, b, (((1,), (1,)), ((), ())), preferred_element_type=F32)  23.1 us
    pallas_call x1, Pallas kernels, attend_back(): pl.pallas_call(attend_back_kernel, grid_spec=grid, out_shape=(jax.ShapeDt...  22.9 us
    unnamed x110, local copies, waits for them, and re-layouts  17.2 us
    pallas_call x1, Pallas kernels, attend(): pl.pallas_call(attend_kernel, grid_spec=grid, out_shape=(jax.ShapeDtypeSt...  16.9 us
  transfers between devices with their start and end apart: 78, of which 33 were waited for; matrix products, arithmetic and copies ran while one was open for 23% of the time, Pallas kernels for 11%

profile of v1, /device:TPU:0, one launch (start us, length us, event | category | flops | bytes accessed | tf_op | source)
XLA Modules:
  0.0 427.0 jit_solution(13085182001505388502)
XLA Ops:
  60.2 5.4 %shard_map.203 = (bf16[512,512]{1,0:T(8,128)(2,1)}, bf16[512,128]{1,0:T(8,128)(2,1)}) custom-call(bf16[512,2048]{1,0:T(8,128)(2,1)} %constant_dynamic-update-slice_fusion.x_ref, bf16[2048,1152]{1,0:T(8,128)(2,1)} %all-gather.3.cloned.1.call-done.w_ref, f32[512,128]{1,0:T(8,128)} %get-tuple-element.108.cos_ref, f32[512,128]{1,0:T(8,128)} %get-tuple-element.109.sin_ref), custom_call_target="tpu_custom_call" | custom-call | flops 1342177280 | bytes 6291456 | tf_op jit(solution)/shard_map/pallas_call | solution.py:146
  71.7 5.2 %collective-permute-done.6.kv0_ref = bf16[512,128]{1,0:T(8,128)(2,1)S(1)} collective-permute-done((bf16[512,128]{1,0:T(8,128)(2,1)}, bf16[512,128]{1,0:T(8,128)(2,1)S(1)}, u32[]{:S(2)}, u32[]{:S(2)}) %collective-permute-start.6) | collective-permute-done | bytes 131104 | tf_op jit(solution)/shard_map/ppermute | solution.py:108
  77.6 16.9 %shard_map.204 = (bf16[512,512]{1,0:T(8,128)(2,1)}, f32[4,2,512]{2,1,0:T(2,128)}) custom-call(s32[1]{0:T(128)} %bitcast.place_ref, bf16[512,512]{1,0:T(8,128)(2,1)} %get-tuple-element.17.q_ref, bf16[512,128]{1,0:T(8,128)(2,1)} %copy-done.42, bf16[512,128]{1,0:T(8,128)(2,1)} %copy-done.41, bf16[512,128]{1,0:T(8,128)(2,1)} %get-tuple-element.18.kv2_ref, ...), custom_call_target="tpu_custom_call" | custom-call | flops 2684354560 | bytes 4194304 | tf_op jit(solution)/shard_map/pallas_call | solution.py:256
  113.9 3.7 collective-permute-done.9
  126.8 5.7 %collective-permute-done.15 = bf16[64,2048]{1,0:T(8,128)(2,1)S(1)} collective-permute-done((bf16[64,2048]{1,0:T(8,128)(2,1)S(1)}, bf16[64,2048]{1,0:T(8,128)(2,1)S(1)}, u32[]{:S(2)}, u32[]{:S(2)}) %collective-permute-start.15) | collective-permute-done | bytes 262176 | tf_op jit(solution)/shard_map/ppermute | solution.py:34
  137.5 6.1 %collective-permute-done.17 = bf16[64,2048]{1,0:T(8,128)(2,1)S(1)} collective-permute-done((bf16[64,2048]{1,0:T(8,128)(2,1)S(1)}, bf16[64,2048]{1,0:T(8,128)(2,1)S(1)}, u32[]{:S(2)}, u32[]{:S(2)}) %collective-permute-start.17) | collective-permute-done | bytes 262176 | tf_op jit(solution)/shard_map/ppermute | solution.py:34
  146.6 8.4 %fusion.2 = f32[512,1408]{1,0:T(8,128)} fusion(bf16[512,2048]{1,0:T(8,128)(2,1)} %constant_dynamic-update-slice_fusion.7.normed_ref, bf16[2048,4224]{1,0:T(8,128)(2,1)} %all-gather.5.cloned.1.call-done), kind=kOutput, calls=%fused_computation.2 | convolution fusion | flops 2952790016 | bytes 10747904 | tf_op jit(solution)/shard_map/dot_general | solution.py:21
  156.5 5.1 %fusion.6 = f32[512,1408]{1,0:T(8,128)} fusion(bf16[512,2048]{1,0:T(8,128)(2,1)S(1)} %copy-done.26, bf16[2048,4224]{1,0:T(8,128)(2,1)S(1)} %copy-done.40), kind=kOutput, calls=%fused_computation.7 | convolution fusion | flops 2952790016 | bytes 10747904 | tf_op jit(solution)/shard_map/dot_general | solution.py:21
  161.5 8.1 %multiply_convert_fusion.1 = (bf16[512,1408]{1,0:T(8,128)(2,1)S(1)}, bf16[512,1408]{1,0:T(8,128)(2,1)S(1)}, bf16[512,1408]{1,0:T(8,128)(2,1)}) fusion(f32[512,1408]{1,0:T(8,128)} %fusion.6, f32[512,1408]{1,0:T(8,128)} %fusion.2, bf16[512,2048]{1,0:T(8,128)(2,1)} %constant_dynamic-update-slice_fusion.7.normed_ref, bf16[2048,4224]{1,0:T(8,128)(2,1)S(1)} %copy-done.40), kind=kOutput, calls=%fused_computation.21 | convolution fusion | flops 2963603456 | bytes 17956864 | tf_op jit(solution)/shard_map/dot_general | solution.py:21
  172.2 26.3 %shard_map.206 = bf16[2048,4224]{1,0:T(8,128)(2,1)} custom-call(bf16[512,2048]{1,0:T(8,128)(2,1)} %constant_dynamic-update-slice_fusion.7.normed_ref, bf16[512,2048]{1,0:T(8,128)(2,1)} %constant_dynamic-update-slice_fusion.14.dy_ref, bf16[512,2816]{1,0:T(8,128)(2,1)} %pad_maximum_fusion.1.dgu_ref, bf16[512,1408]{1,0:T(8,128)(2,1)} %get-tuple-element.33.act_ref), custom_call_target="tpu_custom_call" | custom-call | flops 8858370048 | bytes 31457280 | tf_op jit(solution)/shard_map/pallas_call | solution.py:390
  198.6 6.6 %fusion.14 = bf16[512,2048]{1,0:T(8,128)(2,1)S(1)} fusion(bf16[512,1408]{1,0:T(8,128)(2,1)} %get-tuple-element.33.act_ref, bf16[2048,4224]{1,0:T(8,128)(2,1)} %all-gather.5.cloned.1.call-done), kind=kOutput, calls=%fused_computation.17 | convolution fusion | flops 2953838592 | bytes 9306112 | tf_op jit(solution)/shard_map/dot_general | solution.py:25
  208.9 9.6 %fusion.11 = bf16[512,2048]{1,0:T(8,128)(2,1)S(1)} fusion(bf16[2048,4224]{1,0:T(8,128)(2,1)} %all-gather.5.cloned.1.call-done, bf16[512,1408]{1,0:T(8,128)(2,1)S(1)} %copy-done.17, bf16[512,1408]{1,0:T(8,128)(2,1)S(1)} %copy-done.15), kind=kOutput, calls=%fused_computation.14 | convolution fusion | flops 5912395776 | bytes 16515072 | tf_op jit(solution)/shard_map/dot_general | solution.py:25
  222.2 6.6 %collective-permute-done.32 = bf16[64,2048]{1,0:T(8,128)(2,1)S(1)} collective-permute-done((bf16[64,2048]{1,0:T(8,128)(2,1)S(1)}, bf16[64,2048]{1,0:T(8,128)(2,1)S(1)}, u32[]{:S(2)}, u32[]{:S(2)}) %collective-permute-start.32) | collective-permute-done | bytes 262176 | tf_op jit(solution)/shard_map/ppermute | solution.py:34
  259.6 3.7 collective-permute-start.42
  263.6 7.5 %collective-permute-done.41 = bf16[64,2048]{1,0:T(8,128)(2,1)S(1)} collective-permute-done((bf16[64,2048]{1,0:T(8,128)(2,1)S(1)}, bf16[64,2048]{1,0:T(8,128)(2,1)S(1)}, u32[]{:S(2)}, u32[]{:S(2)}) %collective-permute-start.41) | collective-permute-done | bytes 262176 | tf_op jit(solution)/shard_map/ppermute | solution.py:34
  271.2 3.8 fusion.26.do_ref
  275.0 22.9 %shard_map.205 = (bf16[512,512]{1,0:T(8,128)(2,1)}, f32[3,512,128]{2,1,0:T(8,128)}) custom-call(s32[1]{0:T(128)} %bitcast.place_ref, bf16[512,512]{1,0:T(8,128)(2,1)} %get-tuple-element.17.q_ref, bf16[512,512]{1,0:T(8,128)(2,1)} %fusion.26.do_ref, f32[4,2,512]{2,1,0:T(2,128)} %get-tuple-element.20.lse_ref, bf16[512,128]{1,0:T(8,128)(2,1)} %copy-done.42, ...), custom_call_target="tpu_custom_call" | custom-call | flops 6710886400 | bytes 6291456 | tf_op jit(solution)/shard_map/pallas_call | solution.py:360
  304.3 9.3 %collective-permute-done.45 = bf16[512,128]{1,0:T(8,128)(2,1)S(1)} collective-permute-done((bf16[512,128]{1,0:T(8,128)(2,1)S(1)}, bf16[512,128]{1,0:T(8,128)(2,1)S(1)}, u32[]{:S(2)}, u32[]{:S(2)}) %collective-permute-start.45) | collective-permute-done | bytes 131104 | tf_op jit(solution)/shard_map/ppermute | solution.py:108
  315.2 4.8 %fusion.98 = (bf16[2048,640]{0,1:T(8,128)(2,1)}, f32[2048,640]{0,1:T(8,128)}) fusion(bf16[512,2048]{1,0:T(8,128)(2,1)S(1)} %copy-done.3, bf16[512,64]{1,0:T(8,128)(2,1)S(1)} %slice.488, bf16[512,64]{1,0:T(8,128)(2,1)S(1)} %fusion.58, bf16[512,512]{1,0:T(8,128)(2,1)S(1)} %copy-done.20), kind=kOutput, calls=%fused_computation.222 | convolution fusion | flops 1345454080 | bytes 10616832 | tf_op jit(solution)/shard_map/dot_general | solution.py:29
  320.0 5.9 %copy.28 = f32[2048,640]{1,0:T(8,128)} copy(f32[2048,640]{0,1:T(8,128)} %get-tuple-element.107) | data formatting | bytes 10485760 | tf_op jit(solution)/shard_map/dot_general | solution.py:29
  326.0 3.9 multiply_reduce_fusion
  332.3 3.7 convolution_convert_fusion.2
  350.4 6.8 %copy.27 = bf16[2048,1152]{1,0:T(8,128)(2,1)} copy(bf16[2048,1152]{0,1:T(8,128)(2,1)} %pad_maximum_fusion) | data formatting | bytes 9437184 | tf_op jit(solution)/shard_map/concatenate | solution.py:500
  395.8 4.8 %collective-permute-done.61 = bf16[4,32,1152]{2,1,0:T(8,128)(2,1)S(1)} collective-permute-done((bf16[4,32,1152]{2,1,0:T(8,128)(2,1)S(1)}, bf16[4,32,1152]{2,1,0:T(8,128)(2,1)S(1)}, u32[]{:S(2)}, u32[]{:S(2)}) %collective-permute-start.61) | collective-permute-done | bytes 294944 | tf_op jit(solution)/shard_map/ppermute | solution.py:34
  (338 shorter events, 220.7 us)
Async XLA Ops:
  7.2 53.0 %all-gather.3.cloned.1.call-start = ((), (), s32[]{:S(2)}) async-start(), calls=%async_computation.1 | async-start | bytes 4866048 | tf_op jit(solution)/shard_map/all_gather | solution.py:426
  9.0 137.6 %all-gather.5.cloned.1.call-start = ((), (), s32[]{:S(2)}) async-start(), calls=%async_computation.2 | async-start | bytes 17842176 | tf_op jit(solution)/shard_map/all_gather | solution.py:429
  11.1 406.9 %reduce-scatter.2.cloned.1.call-start = ((), (), s32[]{:S(2)}) async-start(), calls=%async_computation.3 | async-start | bytes 17842176 | tf_op jit(solution)/shard_map/reduce_scatter | solution.py:473
  11.9 112.9 %collective-permute-start.31 = (bf16[64,2048]{1,0:T(8,128)(2,1)}, bf16[64,2048]{1,0:T(8,128)(2,1)}, u32[]{:S(2)}, u32[]{:S(2)}) collective-permute-start(bf16[64,2048]{1,0:T(8,128)(2,1)} %get-tuple-element.81), channel_id=1, source_target_pairs={{0,32},{32,64},{64,96},{96,0},{1,33},{33,65},{65,97},{97,1},{2,34}... | collective-permute-start | bytes 786440 | tf_op jit(solution)/shard_map/ppermute | solution.py:34
  13.9 29.2 %collective-permute-start.27 = (bf16[64,2048]{1,0:T(8,128)(2,1)}, bf16[64,2048]{1,0:T(8,128)(2,1)S(1)}, u32[]{:S(2)}, u32[]{:S(2)}) collective-permute-start(bf16[64,2048]{1,0:T(8,128)(2,1)} %get-tuple-element.81), channel_id=1, source_target_pairs={{0,96},{32,0},{64,32},{96,64},{1,97},{33,1},{65,33},{97,65},{2,98}... | collective-permute-start | bytes 786440 | tf_op jit(solution)/shard_map/ppermute | solution.py:34
  18.1 18.4 %collective-permute-start.2 = (bf16[64,2048]{1,0:T(8,128)(2,1)}, bf16[64,2048]{1,0:T(8,128)(2,1)S(1)}, u32[]{:S(2)}, u32[]{:S(2)}) collective-permute-start(bf16[64,2048]{1,0:T(8,128)(2,1)} %get-tuple-element.86), channel_id=1, source_target_pairs={{0,32},{32,64},{64,96},{96,0},{1,33},{33,65},{65,97},{97,1},{2,34}... | collective-permute-start | bytes 786440 | tf_op jit(solution)/shard_map/ppermute | solution.py:34
  36.5 14.1 %collective-permute-start.3 = (bf16[64,2048]{1,0:T(8,128)(2,1)S(1)}, bf16[64,2048]{1,0:T(8,128)(2,1)S(1)}, u32[]{:S(2)}, u32[]{:S(2)}) collective-permute-start(bf16[64,2048]{1,0:T(8,128)(2,1)S(1)} %collective-permute-done.2), channel_id=1, source_target_pairs={{0,32},{32,64},{64,96},{96,0},{1,33},{33,65},{65,97},{97,1},{2,34}... | collective-permute-start | bytes 786440 | tf_op jit(solution)/shard_map/ppermute | solution.py:34
  45.3 57.4 %collective-permute-start.30 = (bf16[64,2048]{1,0:T(8,128)(2,1)S(1)}, bf16[64,2048]{1,0:T(8,128)(2,1)S(1)}, u32[]{:S(2)}, u32[]{:S(2)}) collective-permute-start(bf16[64,2048]{1,0:T(8,128)(2,1)S(1)} %collective-permute-done.27), channel_id=1, source_target_pairs={{0,96},{32,0},{64,32},{96,64},{1,97},{33,1},{65,33},{97,65},{2,98}... | collective-permute-start | bytes 786440 | tf_op jit(solution)/shard_map/ppermute | solution.py:34
  50.7 50.3 %collective-permute-start.29 = (bf16[64,2048]{1,0:T(8,128)(2,1)S(1)}, bf16[64,2048]{1,0:T(8,128)(2,1)}, u32[]{:S(2)}, u32[]{:S(2)}) collective-permute-start(bf16[64,2048]{1,0:T(8,128)(2,1)S(1)} %collective-permute-done.28), channel_id=1, source_target_pairs={{0,32},{32,64},{64,96},{96,0},{1,33},{33,65},{65,97},{97,1},{2,34}... | collective-permute-start | bytes 786440 | tf_op jit(solution)/shard_map/ppermute | solution.py:34
  119.1 16.6 %collective-permute-start.16 = (bf16[64,2048]{1,0:T(8,128)(2,1)S(1)}, bf16[64,2048]{1,0:T(8,128)(2,1)S(1)}, u32[]{:S(2)}, u32[]{:S(2)}) collective-permute-start(bf16[64,2048]{1,0:T(8,128)(2,1)S(1)} %get-tuple-element.84), channel_id=1, source_target_pairs={{0,32},{32,64},{64,96},{96,0},{1,33},{33,65},{65,97},{97,1},{2,34}... | collective-permute-start | bytes 786440 | tf_op jit(solution)/shard_map/ppermute | solution.py:34
  120.5 15.6 %collective-permute-start.14 = (bf16[64,2048]{1,0:T(8,128)(2,1)S(1)}, bf16[64,2048]{1,0:T(8,128)(2,1)S(1)}, u32[]{:S(2)}, u32[]{:S(2)}) collective-permute-start(bf16[64,2048]{1,0:T(8,128)(2,1)S(1)} %get-tuple-element.84), channel_id=1, source_target_pairs={{0,96},{32,0},{64,32},{96,64},{1,97},{33,1},{65,33},{97,65},{2,98}... | collective-permute-start | bytes 786440 | tf_op jit(solution)/shard_map/ppermute | solution.py:34
  126.5 19.3 %collective-permute-start.19 = (bf16[64,2048]{1,0:T(8,128)(2,1)S(1)}, bf16[64,2048]{1,0:T(8,128)(2,1)S(1)}, u32[]{:S(2)}, u32[]{:S(2)}) collective-permute-start(bf16[64,2048]{1,0:T(8,128)(2,1)S(1)} %get-tuple-element.83), channel_id=1, source_target_pairs={{0,32},{32,64},{64,96},{96,0},{1,33},{33,65},{65,97},{97,1},{2,34}... | collective-permute-start | bytes 786440 | tf_op jit(solution)/shard_map/ppermute | solution.py:34
  205.4 27.2 %collective-permute-start.20 = (bf16[64,2048]{1,0:T(8,128)(2,1)S(1)}, bf16[64,2048]{1,0:T(8,128)(2,1)S(1)}, u32[]{:S(2)}, u32[]{:S(2)}) collective-permute-start(bf16[64,2048]{1,0:T(8,128)(2,1)S(1)} %get-tuple-element.50), channel_id=1, source_target_pairs={{0,32},{32,64},{64,96},{96,0},{1,33},{33,65},{65,97},{97,1},{2,34}... | collective-permute-start | bytes 786440 | tf_op jit(solution)/shard_map/ppermute | solution.py:34
  205.5 27.2 %collective-permute-start.24 = (bf16[64,2048]{1,0:T(8,128)(2,1)S(1)}, bf16[64,2048]{1,0:T(8,128)(2,1)S(1)}, u32[]{:S(2)}, u32[]{:S(2)}) collective-permute-start(bf16[64,2048]{1,0:T(8,128)(2,1)S(1)} %get-tuple-element.51), channel_id=1, source_target_pairs={{0,96},{32,0},{64,32},{96,64},{1,97},{33,1},{65,33},{97,65},{2,98}... | collective-permute-start | bytes 786440 | tf_op jit(solution)/shard_map/ppermute | solution.py:34
  208.7 39.9 %collective-permute-start.23 = (bf16[64,2048]{1,0:T(8,128)(2,1)S(1)}, bf16[64,2048]{1,0:T(8,128)(2,1)S(1)}, u32[]{:S(2)}, u32[]{:S(2)}) collective-permute-start(bf16[64,2048]{1,0:T(8,128)(2,1)S(1)} %get-tuple-element.52), channel_id=1, source_target_pairs={{0,32},{32,64},{64,96},{96,0},{1,33},{33,65},{65,97},{97,1},{2,34}... | collective-permute-start | bytes 786440 | tf_op jit(solution)/shard_map/ppermute | solution.py:34
  247.3 23.9 %collective-permute-start.43 = (bf16[64,2048]{1,0:T(8,128)(2,1)S(1)}, bf16[64,2048]{1,0:T(8,128)(2,1)S(1)}, u32[]{:S(2)}, u32[]{:S(2)}) collective-permute-start(bf16[64,2048]{1,0:T(8,128)(2,1)S(1)} %get-tuple-element.79), channel_id=1, source_target_pairs={{0,32},{32,64},{64,96},{96,0},{1,33},{33,65},{65,97},{97,1},{2,34}... | collective-permute-start | bytes 786440 | tf_op jit(solution)/shard_map/ppermute | solution.py:34
  338.4 31.6 %collective-permute-start.46 = (bf16[64,2048]{1,0:T(8,128)(2,1)}, bf16[64,2048]{1,0:T(8,128)(2,1)S(1)}, u32[]{:S(2)}, u32[]{:S(2)}) collective-permute-start(bf16[64,2048]{1,0:T(8,128)(2,1)} %get-tuple-element.38), channel_id=1, source_target_pairs={{0,32},{32,64},{64,96},{96,0},{1,33},{33,65},{65,97},{97,1},{2,34}... | collective-permute-start | bytes 786440 | tf_op jit(solution)/shard_map/ppermute | solution.py:34
  339.9 30.0 %collective-permute-start.50 = (bf16[64,2048]{1,0:T(8,128)(2,1)}, bf16[64,2048]{1,0:T(8,128)(2,1)}, u32[]{:S(2)}, u32[]{:S(2)}) collective-permute-start(bf16[64,2048]{1,0:T(8,128)(2,1)} %get-tuple-element.39), channel_id=1, source_target_pairs={{0,96},{32,0},{64,32},{96,64},{1,97},{33,1},{65,33},{97,65},{2,98}... | collective-permute-start | bytes 786440 | tf_op jit(solution)/shard_map/ppermute | solution.py:34
  341.7 15.5 %collective-permute-start.70 = (f32[2,2048]{1,0:T(2,128)S(1)}, f32[2,2048]{1,0:T(2,128)S(1)}, u32[]{:S(2)}, u32[]{:S(2)}) collective-permute-start(f32[2,2048]{1,0:T(2,128)S(1)} %add_add_fusion.2), channel_id=1, source_target_pairs={{0,16},{8,24},{16,0},{24,8},{1,17},{9,25},{17,1},{25,9},{2,18},{10... | collective-permute-start | bytes 49160 | tf_op jit(solution)/shard_map/ppermute | solution.py:34
  363.8 19.0 %collective-permute-start.52 = (bf16[16,64,1152]{2,1,0:T(8,128)(2,1)S(1)}, bf16[16,64,1152]{2,1,0:T(8,128)(2,1)S(1)}, u32[]{:S(2)}, u32[]{:S(2)}) collective-permute-start(bf16[16,64,1152]{2,1,0:T(8,128)(2,1)S(1)} %dynamic-slice_bitcast_fusion), channel_id=1, source_target_pairs={{0,1},{1,0},{2,3},{3,2},{4,5},{5,4},{6,7},{7,6},{8,9},{9,8},{10,11... | collective-permute-start | bytes 7077896 | tf_op jit(solution)/shard_map/ppermute | solution.py:34
  385.4 15.2 %collective-permute-start.61 = (bf16[4,32,1152]{2,1,0:T(8,128)(2,1)S(1)}, bf16[4,32,1152]{2,1,0:T(8,128)(2,1)S(1)}, u32[]{:S(2)}, u32[]{:S(2)}) collective-permute-start(bf16[4,32,1152]{2,1,0:T(8,128)(2,1)S(1)} %get-tuple-element.63), channel_id=1, source_target_pairs={{0,16},{8,24},{16,0},{24,8},{1,17},{9,25},{17,1},{25,9},{2,18},{10... | collective-permute-start | bytes 884744 | tf_op jit(solution)/shard_map/ppermute | solution.py:34
  391.8 13.3 %collective-permute-start.53 = (bf16[4,32,1152]{2,1,0:T(8,128)(2,1)S(1)}, bf16[4,32,1152]{2,1,0:T(8,128)(2,1)S(1)}, u32[]{:S(2)}, u32[]{:S(2)}) collective-permute-start(bf16[4,32,1152]{2,1,0:T(8,128)(2,1)S(1)} %get-tuple-element.65), channel_id=1, source_target_pairs={{0,2},{2,4},{4,6},{6,0},{1,3},{3,5},{5,7},{7,1},{8,10},{10,12},{12... | collective-permute-start | bytes 884744 | tf_op jit(solution)/shard_map/ppermute | solution.py:34
  392.8 15.3 %collective-permute-start.55 = (bf16[4,32,1152]{2,1,0:T(8,128)(2,1)S(1)}, bf16[4,32,1152]{2,1,0:T(8,128)(2,1)S(1)}, u32[]{:S(2)}, u32[]{:S(2)}) collective-permute-start(bf16[4,32,1152]{2,1,0:T(8,128)(2,1)S(1)} %get-tuple-element.66), channel_id=1, source_target_pairs={{0,4},{2,6},{4,0},{6,2},{1,5},{3,7},{5,1},{7,3},{8,12},{10,14},{12... | collective-permute-start | bytes 884744 | tf_op jit(solution)/shard_map/ppermute | solution.py:34
  394.7 14.3 %collective-permute-start.54 = (bf16[4,32,1152]{2,1,0:T(8,128)(2,1)S(1)}, bf16[4,32,1152]{2,1,0:T(8,128)(2,1)S(1)}, u32[]{:S(2)}, u32[]{:S(2)}) collective-permute-start(bf16[4,32,1152]{2,1,0:T(8,128)(2,1)S(1)} %get-tuple-element.67), channel_id=1, source_target_pairs={{0,6},{2,0},{4,2},{6,4},{1,7},{3,1},{5,3},{7,5},{8,14},{10,8},{12,... | collective-permute-start | bytes 884744 | tf_op jit(solution)/shard_map/ppermute | solution.py:34
  (98 other events, 1026.6 us)
Sparse Core Ops, SparseCore 0:
  10.9 49.2 all-gather.2
  62.4 73.6 all-gather.4
  198.6 120.6 reduce-scatter.1

commit v2 on v1

--- a/solution.py
+++ b/solution.py
@@ -68,39 +68,47 @@
     return jnp.concatenate([top, bottom], 0)
 
 
-def scatter_axis(value, axis, dim):
+def gather_head_direct(rows):
+    ahead, behind, far = shift(rows, "head", -1), shift(rows, "head", 1), shift(rows, "head", 2)
+    return jnp.concatenate([rows, ahead, far, behind], 0)
+
+
+def scatter_head_direct(partial):
+    n = partial.shape[0] // 4
+    own, ahead, far, behind = (partial[k * n : (k + 1) * n] for k in range(4))
+    ahead, behind, far = shift(ahead, "head", 1), shift(behind, "head", -1), shift(far, "head", 2)
+    return (own.astype(F32) + far.astype(F32)) + (ahead.astype(F32) + behind.astype(F32))
+
+
+def scatter_axis(value, extra, axis):
     index = lax.axis_index(axis)
-
-    def pick(distance):
-        return lax.dynamic_index_in_dim(value, (index + distance) % 4, dim, False)
-
-    ahead, behind, far = (
-        shift(pick(1), axis, 1),
-        shift(pick(3), axis, -1),
-        shift(pick(2), axis, 2),
-    )
-    return pick(0).astype(F32) + ahead.astype(F32) + behind.astype(F32) + far.astype(F32)
-
-
-def scatter_blocks(value):
-    rows = value.shape[0] // 32
-    half = rows // 2
+    rows = value.shape[1]
+
+    def send(distance):
+        piece = lax.dynamic_index_in_dim(value, (index + distance) % 4, 0, False)
+        moved = shift(jnp.concatenate([piece, extra], 0), axis, 2 if distance == 2 else distance)
+        return moved.astype(F32)
+
+    own = jnp.concatenate([lax.dynamic_index_in_dim(value, index, 0, False), extra], 0)
+    total = (own.astype(F32) + send(1)) + (send(-1) + send(2))
+    return total[:rows], total[rows:]
+
+
+def scatter_blocks(value, extra):
+    columns = value.shape[1]
     core = lax.axis_index("core")
-    shaped = value.reshape(16, 2, rows, value.shape[1])
+    shaped = value.reshape(16, 2, 64, columns)
     other = shift(lax.dynamic_index_in_dim(shaped, 1 - core, 1, False), "core", 1)
     pair = add_low(lax.dynamic_index_in_dim(shaped, core, 1, False), other)
-    pair = pair.reshape(4, 4, rows, value.shape[1])
-    first = scatter_axis(pair[:, :, :half], "x", 1).astype(BF16)
-    second = scatter_axis(pair[:, :, half:], "y", 0).astype(BF16)
-    first = scatter_axis(first, "y", 0)
-    second = scatter_axis(second, "x", 0)
-    return jnp.concatenate([first, second], 0)
-
-
-def sum_everywhere(value):
-    for axis in ("head", "y", "x"):
-        value = (value + shift(value, axis, 1)) + (shift(value, axis, -1) + shift(value, axis, 2))
-    return value + shift(value, "core", 1)
+    extra = extra + shift(extra, "core", 1)
+    pair = pair.reshape(4, 4, 64, columns).transpose(1, 0, 2, 3).reshape(4, 256, columns)
+    part, extra = scatter_axis(pair, extra.astype(BF16), "x")
+    part = part.astype(BF16).reshape(4, 64, columns)
+    return scatter_axis(part, extra.astype(BF16), "y")
+
+
+def sum_head(value):
+    return (value + shift(value, "head", 1)) + (shift(value, "head", -1) + shift(value, "head", 2))
 
 
 def from_block(value, distance):
@@ -129,40 +137,39 @@
     return values * cosine + swapped * sine
 
 
-def project_kernel(x_ref, w_ref, cos_ref, sin_ref, q_ref, kv_ref):
+def project_kv_kernel(x_ref, w_ref, cos_ref, sin_ref, kv_ref):
+    flat = dot_nn(x_ref[...], w_ref[...])
+    turned = turn(flat, cos_ref[...], sin_ref[...])
+    kv_ref[...] = jnp.where(lane_is_low(flat.shape, 128), turned, flat).astype(BF16)
+
+
+def project_q_kernel(x_ref, w_ref, cos_ref, sin_ref, q_ref):
     cosine, sine = cos_ref[...], sin_ref[...]
-    x = x_ref[...]
-    for start in (0, 256):
-        wide = dot_nn(x, w_ref[:, start : start + 256])
-        for part in (0, 128):
-            turned = turn(wide[:, part : part + 128], cosine, sine)
-            q_ref[:, start + part : start + part + 128] = (turned * HEAD_SIZE**-0.5).astype(BF16)
-    last = dot_nn(x, w_ref[:, 512:640])
-    kv_ref[...] = jnp.where(lane_is_low(last.shape, 128), turn(last, cosine, sine), last).astype(BF16)
-
-
-def project(normed, weights, cosine, sine):
+    wide = dot_nn(x_ref[...], w_ref[...])
+    for part in (0, 128):
+        turned = turn(wide[:, part : part + 128], cosine, sine)
+        q_ref[:, part : part + 128] = (turned * HEAD_SIZE**-0.5).astype(BF16)
+
+
+def project(kernel, normed, weights, cosine, sine, start, columns, tile):
     rows, width = normed.shape
+    whole = lambda i: (0, 0)
     return pl.pallas_call(
-        project_kernel,
-        out_shape=(
-            jax.ShapeDtypeStruct((rows, 512), BF16),
-            jax.ShapeDtypeStruct((rows, 128), BF16),
-        ),
-        grid=(1,),
+        kernel,
+        out_shape=jax.ShapeDtypeStruct((rows, columns), BF16),
+        grid=(columns // tile,),
         in_specs=[
-            pl.BlockSpec((rows, width), lambda i: (0, 0)),
-            pl.BlockSpec((width, 640), lambda i: (0, 0)),
-            pl.BlockSpec((rows, 128), lambda i: (0, 0)),
-            pl.BlockSpec((rows, 128), lambda i: (0, 0)),
+            pl.BlockSpec((rows, width), whole),
+            pl.BlockSpec((width, tile), lambda i: (0, start // tile + i)),
+            pl.BlockSpec((rows, 128), whole),
+            pl.BlockSpec((rows, 128), whole),
         ],
-        out_specs=(
-            pl.BlockSpec((rows, 512), lambda i: (0, 0)),
-            pl.BlockSpec((rows, 128), lambda i: (0, 0)),
-        ),
+        out_specs=pl.BlockSpec((rows, tile), lambda i: (0, i)),
         compiler_params=pltpu.CompilerParams(vmem_limit_bytes=VMEM_LIMIT),
         cost_estimate=pl.CostEstimate(
-            flops=2 * rows * width * 640, bytes_accessed=6 * 1024 * 1024, transcendentals=0
+            flops=2 * rows * width * columns,
+            bytes_accessed=2 * (rows * width + width * columns + rows * columns),
+            transcendentals=0,
         ),
     )(normed, weights, cosine, sine)
 
@@ -280,7 +287,8 @@
     cos_ref,
     sin_ref,
     dq_ref,
-    dkv_ref,
+    own_ref,
+    earlier_ref,
     kk,
     vv,
     kvt,
@@ -330,7 +338,11 @@
                 key, value = dk[frm, :], dv[frm, :]
                 key = key + pltpu.roll(key, 64, 1)
                 value = value + pltpu.roll(value, 64, 1)
-                dkv_ref[block, pl.ds(at, 128), :] = jnp.where(half, key, value)
+                both = jnp.where(half, key, value)
+                if block == 2:
+                    own_ref[pl.ds(at, 128), :] = both
+                else:
+                    earlier_ref[block, pl.ds(at, 128), :] = both.astype(BF16)
 
 
 def attend_back(place, queries, grad_attended, lse, kv, qseg, kseg, cosine, sine):
@@ -352,7 +364,8 @@
         ],
         out_specs=(
             pl.BlockSpec((512, 128), lambda p, s: (0, p)),
-            pl.BlockSpec((3, 512, 128), lambda p, s: (0, 0, 0)),
+            pl.BlockSpec((512, 128), whole),
+            pl.BlockSpec((2, 512, 128), lambda p, s: (0, 0, 0)),
         ),
         scratch_shapes=ATTENTION_SCRATCH
         + [pltpu.VMEM((1536, 128), F32), pltpu.VMEM((1536, 128), F32)],
@@ -362,7 +375,8 @@
         grid_spec=grid,
         out_shape=(
             jax.ShapeDtypeStruct((512, 512), BF16),
-            jax.ShapeDtypeStruct((3, 512, 128), F32),
+            jax.ShapeDtypeStruct((512, 128), F32),
+            jax.ShapeDtypeStruct((2, 512, 128), BF16),
         ),
         compiler_params=pltpu.CompilerParams(vmem_limit_bytes=VMEM_LIMIT),
         cost_estimate=pl.CostEstimate(
@@ -371,38 +385,166 @@
     )(place, queries, grad_attended, lse, *kv, qseg, kseg, cosine, sine)
 
 
-def weight_grad_kernel(normed_ref, dy_ref, dgu_ref, act_ref, out_ref):
-    part = pl.program_id(0)
-
-    @pl.when(part < 2)
-    def _():
-        out_ref[...] = dot_tn(normed_ref[...], dgu_ref[...]).astype(BF16)
-
-    @pl.when(part == 2)
-    def _():
-        out_ref[...] = dot_tn(dy_ref[...], act_ref[...]).astype(BF16)
-
-
-def weight_grads(normed, dy, dgu, act):
+HIDDEN = 1408
+GROUPS = [(0, 256), (256, 256), (512, 256), (768, 256), (1024, 256), (1280, 128)]
+
+
+def ffn_kernel(x_ref, dy_ref, w_ref, act_ref, dgu_ref, dx_ref, held, sems):
+    copies = []
+    for number, (start, width) in enumerate(GROUPS):
+        for part in range(3):
+            columns = pl.ds(part * HIDDEN + start, width)
+            copy = pltpu.make_async_copy(
+                w_ref.at[:, columns], held.at[:, columns], sems.at[3 * number + part]
+            )
+            copy.start()
+            copies.append(copy)
+    x, dy = x_ref[...], dy_ref[...]
+    for number, (start, width) in enumerate(GROUPS):
+        for part in range(3):
+            copies[3 * number + part].wait()
+        gate = dot_nn(x, held[:, start : start + width])
+        up = dot_nn(x, held[:, HIDDEN + start : HIDDEN + start + width])
+        dact = dot_nn(dy, held[:, 2 * HIDDEN + start : 2 * HIDDEN + start + width])
+        sig = jax.nn.sigmoid(gate)
+        silu = gate * sig
+        act_ref[:, start : start + width] = (silu * up).astype(BF16)
+        dgate = dact * up * (sig * (1.0 + gate * (1.0 - sig)))
+        dgu_ref[:, start : start + width] = dgate.astype(BF16)
+        dgu_ref[:, HIDDEN + start : HIDDEN + start + width] = (dact * silu).astype(BF16)
+    dgu = dgu_ref[...]
+    for start in range(0, 2048, 512):
+        dx = dot_nt(dgu, held[start : start + 512, : 2 * HIDDEN])
+        dx_ref[:, start : start + 512] = dx.astype(BF16)
+
+
+def ffn(normed, dy, weights):
     rows, width = normed.shape
-    hidden = act.shape[1]
-    tile = 256
+    vmem = pl.BlockSpec(memory_space=pltpu.VMEM)
+    return pl.pallas_call(
+        ffn_kernel,
+        out_shape=(
+            jax.ShapeDtypeStruct((rows, HIDDEN), BF16),
+            jax.ShapeDtypeStruct((rows, 2 * HIDDEN), BF16),
+            jax.ShapeDtypeStruct((rows, width), BF16),
+        ),
+        in_specs=[vmem, vmem, pl.BlockSpec(memory_space=pl.ANY)],
+        out_specs=(vmem, vmem, vmem),
+        scratch_shapes=[pltpu.VMEM((width, 3 * HIDDEN), BF16), pltpu.SemaphoreType.DMA((18,))],
+        compiler_params=pltpu.CompilerParams(vmem_limit_bytes=VMEM_LIMIT),
+        cost_estimate=pl.CostEstimate(
+            flops=10 * rows * width * HIDDEN,
+            bytes_accessed=28 * 1024 * 1024,
+            transcendentals=rows * HIDDEN,
+        ),
+    )(normed, dy, weights)
+
+
+def weight_grad_kernel(*refs):
+    left_ref, right_ref, out_ref = refs[-3:]
+    out_ref[...] = dot_tn(left_ref[...], right_ref[...]).astype(BF16)
+
+
+def weight_grad(held, left, right, right_part, part):
+    rows, width = left.shape
+    tile = 512
+    specs = [
+        pl.BlockSpec((rows, tile), lambda i: (0, i)),
+        pl.BlockSpec((rows, HIDDEN), lambda i: (0, right_part)),
+    ]
+    operands = (left, right)
+    if held is not None:
+        specs = [pl.BlockSpec(memory_space=pl.ANY)] + specs
+        operands = (held,) + operands
     return pl.pallas_call(
         weight_grad_kernel,
-        out_shape=jax.ShapeDtypeStruct((width, 3 * hidden), BF16),
-        grid=(3, width // tile),
-        in_specs=[
-            pl.BlockSpec((rows, tile), lambda j, i: (0, i)),
-            pl.BlockSpec((rows, tile), lambda j, i: (0, i)),
-            pl.BlockSpec((rows, hidden), lambda j, i: (0, jnp.minimum(j, 1))),
-            pl.BlockSpec((rows, hidden), lambda j, i: (0, 0)),
-        ],
-        out_specs=pl.BlockSpec((tile, hidden), lambda j, i: (i, j)),
+        out_shape=jax.ShapeDtypeStruct((width, 3 * HIDDEN), BF16),
+        grid=(width // tile,),
+        in_specs=specs,
+        out_specs=pl.BlockSpec((tile, HIDDEN), lambda i: (i, part)),
+        input_output_aliases={} if held is None else {0: 0},
         compiler_params=pltpu.CompilerParams(vmem_limit_bytes=VMEM_LIMIT),
         cost_estimate=pl.CostEstimate(
-            flops=2 * 3 * rows * width * hidden, bytes_accessed=30 * 1024 * 1024, transcendentals=0
-        ),
-    )(normed, dy, dgu, act)
+            flops=2 * rows * width * HIDDEN, bytes_accessed=10 * 1024 * 1024, transcendentals=0
+        ),
+    )(*operands)
+
+
+def rows_times_kernel(left_ref, right_ref, out_ref):
+    out_ref[...] = dot_nt(left_ref[...], right_ref[...]).astype(BF16)
+
+
+def rows_times(left, right, right_part):
+    rows, depth = left.shape
+    width = right.shape[0]
+    tile = 512
+    return pl.pallas_call(
+        rows_times_kernel,
+        out_shape=jax.ShapeDtypeStruct((rows, width), BF16),
+        grid=(width // tile,),
+        in_specs=[
+            pl.BlockSpec((rows, depth), lambda i: (0, 0)),
+            pl.BlockSpec((tile, depth), lambda i: (i, right_part)),
+        ],
+        out_specs=pl.BlockSpec((rows, tile), lambda i: (0, i)),
+        compiler_params=pltpu.CompilerParams(vmem_limit_bytes=VMEM_LIMIT),
+        cost_estimate=pl.CostEstimate(
+            flops=2 * rows * depth * width,
+            bytes_accessed=2 * (rows * depth + width * depth + rows * width),
+            transcendentals=0,
+        ),
+    )(left, right)
+
+
+def finish_kernel(
+    x_ref, w_ref, dq_ref, own_ref, one_ref, two_ref, cos_ref, sin_ref, grad_ref, dx_ref, gain_ref, dqkv
+):
+    dqkv[:, :512] = dq_ref[...]
+    dkv = own_ref[...] + one_ref[...].astype(F32) + two_ref[...].astype(F32)
+    turned = turn(dkv, cos_ref[...], -sin_ref[...])
+    dqkv[:, 512:] = jnp.where(lane_is_low(dkv.shape, 128), turned, dkv).astype(BF16)
+    grads = dqkv[...]
+    for start in range(0, 2048, 512):
+        columns = slice(start, start + 512)
+        x = x_ref[:, columns]
+        dx = dot_nt(grads, w_ref[columns, :])
+        dx_ref[:, columns] = dx.astype(BF16)
+        gain_ref[:, columns] = jnp.sum(dx * x.astype(F32), 0, keepdims=True)
+        grad_ref[columns, :] = dot_tn(x, grads).astype(BF16)
+
+
+def finish(normed, weights, dq, own, one, two, cosine, sine):
+    rows, width = normed.shape
+    whole = lambda i: (0, 0)
+    return pl.pallas_call(
+        finish_kernel,
+        out_shape=(
+            jax.ShapeDtypeStruct((width, 640), BF16),
+            jax.ShapeDtypeStruct((rows, width), BF16),
+            jax.ShapeDtypeStruct((1, width), F32),
+        ),
+        grid=(1,),
+        in_specs=[
+            pl.BlockSpec((rows, width), whole),
+            pl.BlockSpec((width, 640), whole),
+            pl.BlockSpec((rows, 512), whole),
+            pl.BlockSpec((rows, 128), whole),
+            pl.BlockSpec((rows, 128), whole),
+            pl.BlockSpec((rows, 128), whole),
+            pl.BlockSpec((rows, 128), whole),
+            pl.BlockSpec((rows, 128), whole),
+        ],
+        out_specs=(
+            pl.BlockSpec((width, 640), whole),
+            pl.BlockSpec((rows, width), whole),
+            pl.BlockSpec((1, width), whole),
+        ),
+        scratch_shapes=[pltpu.VMEM((rows, 640), BF16)],
+        compiler_params=pltpu.CompilerParams(vmem_limit_bytes=VMEM_LIMIT),
+        cost_estimate=pl.CostEstimate(
+            flops=4 * rows * width * 640, bytes_accessed=11 * 1024 * 1024, transcendentals=0
+        ),
+    )(normed, weights, dq, own, one, two, cosine, sine)
 
 
 def per_device(
@@ -444,60 +586,56 @@
     cosine = jnp.concatenate([cosine] * 4, 1)
     sine = jnp.concatenate([-sine, sine, -sine, sine], 1)
 
-    queries, kv_own = project(normed_one, attention_weights, cosine, sine)
+    kv_own = project(project_kv_kernel, normed_one, attention_weights, cosine, sine, 512, 128, 128)
     kv = (from_block(kv_own, 2), from_block(kv_own, 1), kv_own)
+    queries = project(project_q_kernel, normed_one, attention_weights, cosine, sine, 0, 512, 256)
 
     flat = segments.reshape(-1)
     padded = jnp.concatenate([jnp.full((1024,), -1, jnp.int32), flat])
     qseg = lax.dynamic_slice_in_dim(flat, block * 512, 512, 0).reshape(1, 512)
     kseg = lax.dynamic_slice_in_dim(padded, block * 512, 1536, 0).reshape(1536, 1)
 
+    cotangent_rows, queries = lax.optimization_barrier((cotangent[0], queries))
+    dy = gather_head_direct(cotangent_rows)
     attended, lse = attend(place_array, queries, kv, qseg, kseg)
+    attended, dy = lax.optimization_barrier((attended, dy))
     h1 = x_rows + scatter_head(dot_nt(attended, out_t).astype(BF16))
     scale_two = scale_of(h1)
     normed_two = gather_head((h1 * scale_two * gain_two).astype(BF16))
 
-    dy = gather_head(cotangent[0])
-    gate = dot_nn(normed_two, ffn_weights[:, :1408])
-    up = dot_nn(normed_two, ffn_weights[:, 1408:2816])
-    dact = dot_nn(dy, ffn_weights[:, 2816:])
-    sig = jax.nn.sigmoid(gate)
-    silu = gate * sig
-    act = (silu * up).astype(BF16)
-    dgate = (dact * up * (sig * (1.0 + gate * (1.0 - sig)))).astype(BF16)
-    dup = (dact * silu).astype(BF16)
-    dgu = jnp.concatenate([dgate, dup], 1)
-    output = h1 + scatter_head(dot_nt(act, ffn_weights[:, 2816:]).astype(BF16))
-    dnormed_two = scatter_head(dot_nt(dgu, ffn_weights[:, :2816]).astype(BF16))
-
-    ffn_grads = lax.psum_scatter(
-        weight_grads(normed_two, dy, dgu, act), BLK, scatter_dimension=0, tiled=True
-    )
+    act, dgu, dnormed_two = ffn(normed_two, dy, ffn_weights)
+    dnormed_two = scatter_head(dnormed_two)
+    held = weight_grad(None, normed_two, dgu, 0, 0)
+    held = weight_grad(held, normed_two, dgu, 1, 1)
+    held = weight_grad(held, dy, act, 0, 2)
+    ffn_grads = lax.psum_scatter(held, BLK, scatter_dimension=0, tiled=True)
 
     dh1 = cotangent[0].astype(F32) + norm_backward(h1, scale_two, gain_two, dnormed_two)
     grad_gain_two = jnp.sum(dnormed_two * h1 * scale_two, 0)
     dh1_low = gather_head(dh1.astype(BF16))
     dattended = dot_nn(dh1_low, out_t).astype(BF16)
+
+    late_act, dattended = lax.optimization_barrier((act, dattended))
+    output = h1 + scatter_head_direct(rows_times(late_act, ffn_weights, 2))
+    dq, dkv_own, dkv_earlier = attend_back(
+        place_array, queries, dattended, lse, kv, qseg, kseg, cosine, sine
+    )
+    dq, output = lax.optimization_barrier((dq, output))
+    dkv_one = from_block(dkv_earlier[1], -1)
+    dkv_two = from_block(dkv_earlier[0], -2)
     grad_out_t = dot_tn(dh1_low, attended).astype(BF16)
 
-    dq, dkv = attend_back(place_array, queries, dattended, lse, kv, qseg, kseg, cosine, sine)
-    dkv_own = (
-        dkv[2]
-        + from_block(dkv[1].astype(BF16), -1).astype(F32)
-        + from_block(dkv[0].astype(BF16), -2).astype(F32)
-    )
-    dk_own = dkv_own[:, :64]
-    swapped = jnp.concatenate([dk_own[:, 32:], dk_own[:, :32]], 1)
-    dk_own = dk_own * cosine[:, :64] - swapped * sine[:, :64]
-    dqkv = jnp.concatenate([dq, dk_own.astype(BF16), dkv_own[:, 64:].astype(BF16)], 1)
-
-    qkv_weights = attention_weights[:, :640]
-    dnormed_one = scatter_head(dot_nt(dqkv, qkv_weights).astype(BF16))
+    grad_qkv, dnormed_one, grad_gain_one = finish(
+        normed_one, attention_weights, dq, dkv_own, dkv_one, dkv_two, cosine, sine
+    )
+    grad_gain_one = grad_gain_one[0] / gain_one
+    dnormed_one = scatter_head(dnormed_one)
     grad_inputs = dh1 + norm_backward(x_rows, scale_one, gain_one, dnormed_one)
-    grad_qkv = dot_tn(normed_one, dqkv)
-    grad_gain_one = jnp.sum(grad_qkv * qkv_weights.astype(F32), 1) / gain_one
-    gains = sum_everywhere(jnp.stack([grad_gain_one, grad_gain_two]))
-    attention_grads = scatter_blocks(jnp.concatenate([grad_qkv.astype(BF16), grad_out_t], 1))
+    gains = jnp.pad(jnp.concatenate([grad_gain_one, grad_gain_two]), (0, 16 * 1152 - 4096))
+    attention_grads, gains = scatter_blocks(
+        jnp.concatenate([grad_qkv, grad_out_t], 1), gains.reshape(16, 1152)
+    )
+    gains = sum_head(gains.reshape(-1)[:4096].reshape(2, 2048))
 
     return (
         output.astype(BF16)[None],

time: 435 us -> 407 us (0.936)
  matrix products: 55.9 us -> 10.3 us
  Pallas kernels: 71.6 us -> 111 us
  starting transfers between devices: 114 us -> 94.4 us
  waiting for transfers between devices: 98.2 us -> 111 us
  local copies, waits for them, and re-layouts: 42.9 us -> 33.7 us
    pallas_call x2 -> x8, Pallas kernels: 31.7 us -> 72.1 us  [the longest x1 26 us: ffn(): pl.pallas_call(ffn_kernel, out_shape=(jax.ShapeDtypeStruct((rows, HIDDEN)...]
    dot_general x4 -> x1, matrix products: 25.4 us -> 4.29 us  [dot_nn(): return jnp.dot(a, b, preferred_element_type=F32)]
    dot_general x4 -> x1, matrix products: 23.1 us -> 2.96 us  [dot_nt(): lax.dot_general(a, b, (((1,), (1,)), ((), ())), preferred_element_type=F32)]
    ppermute x71 -> x53, starting transfers between devices: 106 us -> 86.5 us  [shift(): lax.ppermute(value, axis, [(i, (i + distance) % size) for i in range(size)])]
    all_gather x1, waiting for transfers between devices: 3.15 us -> 19.3 us  [per_device(): lax.all_gather(jnp.concatenate([w_query, key_projection, value_projection...]
    ppermute x4, waiting for transfers between devices: 14.5 us -> 4.6 us  [from_block(): return lax.ppermute(value, BLK, route)]
    concatenate x1 -> x0, local copies, waits for them, and re-layouts: 6.75 us -> none  [per_device(): jnp.concatenate([grad_qkv.astype(BF16), grad_out_t], 1)]
    ppermute x71 -> x53, waiting for transfers between devices: 80.5 us -> 86.9 us  [shift(): lax.ppermute(value, axis, [(i, (i + distance) % size) for i in range(size)])]
  transfers between devices with their start and end apart: 78 -> 60, of which waited for: 33 -> 27; matrix products, arithmetic and copies ran while one was open for 23% -> 15% of each run, Pallas kernels for 11% -> 16%
where the time goes in v2:
time: 407 us; the launch traced here: 400 us
  waiting for transfers between devices  111 us (27%)
  Pallas kernels  111 us (27%)
  starting transfers between devices  94.4 us (23%)
  local copies, waits for them, and re-layouts  33.7 us (8%)
  other arithmetic  24.9 us (6%)
  between operations  14.8 us (4%)
  matrix products  10.3 us (3%)
    ppermute x53, waiting for transfers between devices, shift(): lax.ppermute(value, axis, [(i, (i + distance) % size) for i in range(size)])  86.9 us
    ppermute x53, starting transfers between devices, shift(): lax.ppermute(value, axis, [(i, (i + distance) % size) for i in range(size)])  86.5 us
    pallas_call x1, Pallas kernels, ffn(): pl.pallas_call(ffn_kernel, out_shape=(jax.ShapeDtypeStruct((rows, HIDDEN)...  26 us
    pallas_call x1, Pallas kernels, attend_back(): pl.pallas_call(attend_back_kernel, grid_spec=grid, out_shape=(jax.ShapeDt...  22.4 us
    pallas_call x3, Pallas kernels, weight_grad(): pl.pallas_call(weight_grad_kernel, out_shape=jax.ShapeDtypeStruct((width,...  22 us
    all_gather x1, waiting for transfers between devices, per_device(): lax.all_gather(jnp.concatenate([w_query, key_projection, value_projection...  19.3 us
    pallas_call x1, Pallas kernels, attend(): pl.pallas_call(attend_kernel, grid_spec=grid, out_shape=(jax.ShapeDtypeSt...  16.9 us
    unnamed x52, local copies, waits for them, and re-layouts  15.9 us
  transfers between devices with their start and end apart: 60, of which 27 were waited for; matrix products, arithmetic and copies ran while one was open for 15% of the time, Pallas kernels for 16%

profile of v2, /device:TPU:0, one launch (start us, length us, event | category | flops | bytes accessed | tf_op | source)
XLA Modules:
  0.0 400.3 jit_solution(12750329108350115073)
XLA Ops:
  31.3 6.5 %collective-permute-done.3 = bf16[64,2048]{1,0:T(8,128)(2,1)S(1)} collective-permute-done((bf16[64,2048]{1,0:T(8,128)(2,1)S(1)}, bf16[64,2048]{1,0:T(8,128)(2,1)S(1)}, u32[]{:S(2)}, u32[]{:S(2)}) %collective-permute-start.3) | collective-permute-done | bytes 262176 | tf_op jit(solution)/shard_map/ppermute | solution.py:34
  40.7 19.3 %all-gather.3.cloned.1.call-done.w_ref = bf16[2048,1152]{1,0:T(8,128)(2,1)} async-done(((bf16[64,1152]{1,0:T(8,128)(2,1)}), bf16[2048,1152]{1,0:T(8,128)(2,1)}) %all-gather.3.cloned.1.call-update) | async-done | bytes 4718608 | tf_op jit(solution)/shard_map/all_gather | solution.py:568
  60.1 4.6 %shard_map.203.q_ref = bf16[512,512]{1,0:T(8,128)(2,1)} custom-call(bf16[512,2048]{1,0:T(8,128)(2,1)} %constant_dynamic-update-slice_fusion.x_ref, bf16[2048,1152]{1,0:T(8,128)(2,1)} %all-gather.3.cloned.1.call-done.w_ref, f32[512,128]{1,0:T(8,128)} %get-tuple-element.120.cos_ref, f32[512,128]{1,0:T(8,128)} %get-tuple-element.121.sin_ref), custom_call_target="tpu_custom_call" | custom-call | flops 1073741824 | bytes 4718592 | tf_op jit(solution)/shard_map/pallas_call | solution.py:157
  75.3 3.9 collective-permute-start.6
  81.2 4.6 %collective-permute-done.6.kv0_ref = bf16[512,128]{1,0:T(8,128)(2,1)S(1)} collective-permute-done((bf16[512,128]{1,0:T(8,128)(2,1)}, bf16[512,128]{1,0:T(8,128)(2,1)S(1)}, u32[]{:S(2)}, u32[]{:S(2)}) %collective-permute-start.6) | collective-permute-done | bytes 131104 | tf_op jit(solution)/shard_map/ppermute | solution.py:116
  86.4 16.9 %shard_map.205 = (bf16[512,512]{1,0:T(8,128)(2,1)}, f32[4,2,512]{2,1,0:T(2,128)}) custom-call(s32[1]{0:T(128)} %bitcast.place_ref, bf16[512,512]{1,0:T(8,128)(2,1)} %shard_map.203.q_ref, bf16[512,128]{1,0:T(8,128)(2,1)} %copy-done.14, bf16[512,128]{1,0:T(8,128)(2,1)} %copy-done.13, bf16[512,128]{1,0:T(8,128)(2,1)} %shard_map.204.kv2_ref, ...), custom_call_target="tpu_custom_call" | custom-call | flops 2684354560 | bytes 4194304 | tf_op jit(solution)/shard_map/pallas_call | solution.py:263
  123.1 5.6 %collective-permute-done.12 = bf16[64,2048]{1,0:T(8,128)(2,1)S(1)} collective-permute-done((bf16[64,2048]{1,0:T(8,128)(2,1)S(1)}, bf16[64,2048]{1,0:T(8,128)(2,1)S(1)}, u32[]{:S(2)}, u32[]{:S(2)}) %collective-permute-start.12) | collective-permute-done | bytes 262176 | tf_op jit(solution)/shard_map/ppermute | solution.py:34
  140.5 3.7 collective-permute-start.21
  147.6 7.4 %collective-permute-done.20 = bf16[64,2048]{1,0:T(8,128)(2,1)S(1)} collective-permute-done((bf16[64,2048]{1,0:T(8,128)(2,1)S(1)}, bf16[64,2048]{1,0:T(8,128)(2,1)S(1)}, u32[]{:S(2)}, u32[]{:S(2)}) %collective-permute-start.20) | collective-permute-done | bytes 262176 | tf_op jit(solution)/shard_map/ppermute | solution.py:34
  157.8 26.0 %shard_map.206 = (bf16[512,1408]{1,0:T(8,128)(2,1)}, bf16[512,2816]{1,0:T(8,128)(2,1)}, bf16[512,2048]{1,0:T(8,128)(2,1)}) custom-call(bf16[512,2048]{1,0:T(8,128)(2,1)} %constant_dynamic-update-slice_fusion.7.x_ref.refs_0_.refs_1_, bf16[512,2048]{1,0:T(8,128)(2,1)} %pad_maximum_fusion.1.dy_ref.refs_1_, ...), custom_call_target="tpu_custom_call" | custom-call | flops 14763950080 | bytes 29360128 | tf_op jit(solution)/shard_map/pallas_call | solution.py:424
  183.8 7.3 %shard_map.210.refs_0_ = bf16[2048,4224]{1,0:T(8,128)(2,1)} custom-call(bf16[512,2048]{1,0:T(8,128)(2,1)} %constant_dynamic-update-slice_fusion.7.x_ref.refs_0_.refs_1_, bf16[512,2816]{1,0:T(8,128)(2,1)} %get-tuple-element.48.refs_1_.refs_2_), custom_call_target="tpu_custom_call" | custom-call | flops 2952790016 | bytes 10485760 | tf_op jit(solution)/shard_map/pallas_call | solution.py:459
  191.1 7.4 %shard_map.211.refs_0_ = bf16[2048,4224]{1,0:T(8,128)(2,1)} custom-call(bf16[2048,4224]{1,0:T(8,128)(2,1)} %shard_map.210.refs_0_, bf16[512,2048]{1,0:T(8,128)(2,1)} %constant_dynamic-update-slice_fusion.7.x_ref.refs_0_.refs_1_, bf16[512,2816]{1,0:T(8,128)(2,1)} %get-tuple-element.48.refs_1_.refs_2_), custom_call_target="tpu_custom_call", output_to_operand_aliasing={{}: (0, {})} | custom-call | flops 2952790016 | bytes 10485760 | tf_op jit(solution)/shard_map/pallas_call | solution.py:459
  198.5 7.3 %shard_map.212 = bf16[2048,4224]{1,0:T(8,128)(2,1)} custom-call(bf16[2048,4224]{1,0:T(8,128)(2,1)} %shard_map.211.refs_0_, bf16[512,2048]{1,0:T(8,128)(2,1)} %pad_maximum_fusion.1.dy_ref.refs_1_, bf16[512,1408]{1,0:T(8,128)(2,1)} %get-tuple-element.40.left_ref.refs_2_), custom_call_target="tpu_custom_call", output_to_operand_aliasing={{}: (0, {})} | custom-call | flops 2952790016 | bytes 10485760 | tf_op jit(solution)/shard_map/pallas_call | solution.py:459
  213.9 3.9 collective-permute-done.23
  223.4 4.3 %collective-permute-done.24 = bf16[64,2048]{1,0:T(8,128)(2,1)S(1)} collective-permute-done((bf16[64,2048]{1,0:T(8,128)(2,1)S(1)}, bf16[64,2048]{1,0:T(8,128)(2,1)S(1)}, u32[]{:S(2)}, u32[]{:S(2)}) %collective-permute-start.24) | collective-permute-done | bytes 262176 | tf_op jit(solution)/shard_map/ppermute | solution.py:34
  236.4 3.8 collective-permute-done.30
  240.2 3.7 collective-permute-start.33
  255.1 4.3 %fusion.8.do_ref = bf16[512,512]{1,0:T(8,128)(2,1)} fusion(bf16[512,2048]{1,0:T(8,128)(2,1)} %constant_dynamic-update-slice_fusion.14, bf16[2048,1152]{1,0:T(8,128)(2,1)} %all-gather.3.cloned.1.call-done.w_ref), kind=kOutput, calls=%fused_computation.17 | convolution fusion | flops 1074003968 | bytes 4718592 | tf_op jit(solution)/shard_map/dot_general | solution.py:21
  259.4 7.4 %shard_map.208 = bf16[512,2048]{1,0:T(8,128)(2,1)} custom-call(bf16[512,1408]{1,0:T(8,128)(2,1)} %get-tuple-element.40.left_ref.refs_2_, bf16[2048,4224]{1,0:T(8,128)(2,1)} %all-gather.5.cloned.1.call-done.w_ref.right_ref), custom_call_target="tpu_custom_call" | custom-call | flops 2952790016 | bytes 9306112 | tf_op jit(solution)/shard_map/pallas_call | solution.py:481
  271.4 22.4 %shard_map.207 = (bf16[512,512]{1,0:T(8,128)(2,1)}, f32[512,128]{1,0:T(8,128)}, bf16[2,512,128]{2,1,0:T(8,128)(2,1)}) custom-call(s32[1]{0:T(128)} %bitcast.place_ref, bf16[512,512]{1,0:T(8,128)(2,1)} %shard_map.203.q_ref, bf16[512,512]{1,0:T(8,128)(2,1)} %fusion.8.do_ref, f32[4,2,512]{2,1,0:T(2,128)} %get-tuple-element.38.lse_ref, ...), custom_call_target="tpu_custom_call" | custom-call | flops 6710886400 | bytes 6291456 | tf_op jit(solution)/shard_map/pallas_call | solution.py:373
  304.0 8.5 %shard_map.209 = (bf16[2048,640]{1,0:T(8,128)(2,1)}, bf16[512,2048]{1,0:T(8,128)(2,1)}, f32[1,2048]{1,0:T(1,128)}) custom-call(bf16[512,2048]{1,0:T(8,128)(2,1)} %constant_dynamic-update-slice_fusion.x_ref, bf16[2048,1152]{1,0:T(8,128)(2,1)} %all-gather.3.cloned.1.call-done.w_ref, bf16[512,512]{1,0:T(8,128)(2,1)} %get-tuple-element.42.dq_ref, ...), custom_call_target="tpu_custom_call" | custom-call | flops 2684354560 | bytes 11534336 | tf_op jit(solution)/shard_map/pallas_call | solution.py:519
  343.9 3.8 collective-permute-start.50
  348.2 10.1 %collective-permute-done.48 = bf16[272,1152]{1,0:T(8,128)(2,1)S(1)} collective-permute-done((bf16[272,1152]{1,0:T(8,128)(2,1)S(1)}, bf16[272,1152]{1,0:T(8,128)(2,1)S(1)}, u32[]{:S(2)}, u32[]{:S(2)}) %collective-permute-start.48) | collective-permute-done | bytes 626720 | tf_op jit(solution)/shard_map/ppermute | solution.py:34
  360.8 11.3 %collective-permute-done.50 = bf16[272,1152]{1,0:T(8,128)(2,1)S(1)} collective-permute-done((bf16[272,1152]{1,0:T(8,128)(2,1)S(1)}, bf16[272,1152]{1,0:T(8,128)(2,1)S(1)}, u32[]{:S(2)}, u32[]{:S(2)}) %collective-permute-start.50) | collective-permute-done | bytes 626720 | tf_op jit(solution)/shard_map/ppermute | solution.py:34
  (233 shorter events, 181.4 us)
Async XLA Ops:
  7.2 52.9 %all-gather.3.cloned.1.call-start = ((), (), s32[]{:S(2)}) async-start(), calls=%async_computation.1 | async-start | bytes 4866048 | tf_op jit(solution)/shard_map/all_gather | solution.py:568
  9.0 148.9 %all-gather.5.cloned.1.call-start = ((), (), s32[]{:S(2)}) async-start(), calls=%async_computation.2 | async-start | bytes 17842176 | tf_op jit(solution)/shard_map/all_gather | solution.py:571
  11.0 380.3 %reduce-scatter.2.cloned.1.call-start = ((), (), s32[]{:S(2)}) async-start(), calls=%async_computation.3 | async-start | bytes 17842176 | tf_op jit(solution)/shard_map/reduce_scatter | solution.py:611
  12.9 27.1 %collective-permute-start.5 = (bf16[64,2048]{1,0:T(8,128)(2,1)S(1)}, bf16[64,2048]{1,0:T(8,128)(2,1)S(1)}, u32[]{:S(2)}, u32[]{:S(2)}) collective-permute-start(bf16[64,2048]{1,0:T(8,128)(2,1)S(1)} %get-tuple-element.101), channel_id=1, source_target_pairs={{0,32},{32,64},{64,96},{96,0},{1,33},{33,65},{65,97},{97,1},{2,34}... | collective-permute-start | bytes 786440 | tf_op jit(solution)/shard_map/ppermute | solution.py:34
  24.2 14.3 %collective-permute-start.4 = (bf16[64,2048]{1,0:T(8,128)(2,1)S(1)}, bf16[64,2048]{1,0:T(8,128)(2,1)S(1)}, u32[]{:S(2)}, u32[]{:S(2)}) collective-permute-start(bf16[64,2048]{1,0:T(8,128)(2,1)S(1)} %collective-permute-done.1), channel_id=1, source_target_pairs={{0,96},{32,0},{64,32},{96,64},{1,97},{33,1},{65,33},{97,65},{2,98}... | collective-permute-start | bytes 786440 | tf_op jit(solution)/shard_map/ppermute | solution.py:34
  64.7 38.6 %collective-permute-start.10 = (bf16[128,2048]{1,0:T(8,128)(2,1)S(1)}, bf16[128,2048]{1,0:T(8,128)(2,1)S(1)}, u32[]{:S(2)}, u32[]{:S(2)}) collective-permute-start(bf16[128,2048]{1,0:T(8,128)(2,1)S(1)} %bitcast.90), channel_id=1, source_target_pairs={{0,32},{32,64},{64,96},{96,0},{1,33},{33,65},{65,97},{97,1},{2,34}... | collective-permute-start | bytes 1572872 | tf_op jit(solution)/shard_map/ppermute | solution.py:34
  66.2 37.1 %collective-permute-start.9 = (bf16[128,2048]{1,0:T(8,128)(2,1)S(1)}, bf16[128,2048]{1,0:T(8,128)(2,1)S(1)}, u32[]{:S(2)}, u32[]{:S(2)}) collective-permute-start(bf16[128,2048]{1,0:T(8,128)(2,1)S(1)} %bitcast.91), channel_id=1, source_target_pairs={{0,64},{32,96},{64,0},{96,32},{1,65},{33,97},{65,1},{97,33},{2,66}... | collective-permute-start | bytes 1572872 | tf_op jit(solution)/shard_map/ppermute | solution.py:34
  69.1 34.2 %collective-permute-start.8 = (bf16[128,2048]{1,0:T(8,128)(2,1)S(1)}, bf16[128,2048]{1,0:T(8,128)(2,1)S(1)}, u32[]{:S(2)}, u32[]{:S(2)}) collective-permute-start(bf16[128,2048]{1,0:T(8,128)(2,1)S(1)} %bitcast.92), channel_id=1, source_target_pairs={{0,96},{32,0},{64,32},{96,64},{1,97},{33,1},{65,33},{97,65},{2,98}... | collective-permute-start | bytes 1572872 | tf_op jit(solution)/shard_map/ppermute | solution.py:34
  137.0 20.1 %collective-permute-start.22 = (bf16[64,2048]{1,0:T(8,128)(2,1)S(1)}, bf16[64,2048]{1,0:T(8,128)(2,1)S(1)}, u32[]{:S(2)}, u32[]{:S(2)}) collective-permute-start(bf16[64,2048]{1,0:T(8,128)(2,1)S(1)} %get-tuple-element.99), channel_id=1, source_target_pairs={{0,32},{32,64},{64,96},{96,0},{1,33},{33,65},{65,97},{97,1},{2,34}... | collective-permute-start | bytes 786440 | tf_op jit(solution)/shard_map/ppermute | solution.py:34
  140.5 15.2 %collective-permute-start.21 = (bf16[64,2048]{1,0:T(8,128)(2,1)S(1)}, bf16[64,2048]{1,0:T(8,128)(2,1)S(1)}, u32[]{:S(2)}, u32[]{:S(2)}) collective-permute-start(bf16[64,2048]{1,0:T(8,128)(2,1)S(1)} %collective-permute-done.18), channel_id=1, source_target_pairs={{0,96},{32,0},{64,32},{96,64},{1,97},{33,1},{65,33},{97,65},{2,98}... | collective-permute-start | bytes 786440 | tf_op jit(solution)/shard_map/ppermute | solution.py:34
  210.6 12.8 %collective-permute-start.26 = (bf16[64,2048]{1,0:T(8,128)(2,1)S(1)}, bf16[64,2048]{1,0:T(8,128)(2,1)S(1)}, u32[]{:S(2)}, u32[]{:S(2)}) collective-permute-start(bf16[64,2048]{1,0:T(8,128)(2,1)S(1)} %get-tuple-element.76), channel_id=1, source_target_pairs={{0,32},{32,64},{64,96},{96,0},{1,33},{33,65},{65,97},{97,1},{2,34}... | collective-permute-start | bytes 786440 | tf_op jit(solution)/shard_map/ppermute | solution.py:34
  210.6 12.8 %collective-permute-start.25 = (bf16[64,2048]{1,0:T(8,128)(2,1)S(1)}, bf16[64,2048]{1,0:T(8,128)(2,1)S(1)}, u32[]{:S(2)}, u32[]{:S(2)}) collective-permute-start(bf16[64,2048]{1,0:T(8,128)(2,1)S(1)} %get-tuple-element.77), channel_id=1, source_target_pairs={{0,96},{32,0},{64,32},{96,64},{1,97},{33,1},{65,33},{97,65},{2,98}... | collective-permute-start | bytes 786440 | tf_op jit(solution)/shard_map/ppermute | solution.py:34
  236.4 18.0 %collective-permute-start.34 = (bf16[64,2048]{1,0:T(8,128)(2,1)}, bf16[64,2048]{1,0:T(8,128)(2,1)S(1)}, u32[]{:S(2)}, u32[]{:S(2)}) collective-permute-start(bf16[64,2048]{1,0:T(8,128)(2,1)} %get-tuple-element.97), channel_id=1, source_target_pairs={{0,32},{32,64},{64,96},{96,0},{1,33},{33,65},{65,97},{97,1},{2,34}... | collective-permute-start | bytes 786440 | tf_op jit(solution)/shard_map/ppermute | solution.py:34
  240.2 12.7 %collective-permute-start.33 = (bf16[64,2048]{1,0:T(8,128)(2,1)}, bf16[64,2048]{1,0:T(8,128)(2,1)S(1)}, u32[]{:S(2)}, u32[]{:S(2)}) collective-permute-start(bf16[64,2048]{1,0:T(8,128)(2,1)} %collective-permute-done.30), channel_id=1, source_target_pairs={{0,96},{32,0},{64,32},{96,64},{1,97},{33,1},{65,33},{97,65},{2,98}... | collective-permute-start | bytes 786440 | tf_op jit(solution)/shard_map/ppermute | solution.py:34
  269.2 31.3 %collective-permute-start.35 = (bf16[128,2048]{1,0:T(8,128)(2,1)}, bf16[128,2048]{1,0:T(8,128)(2,1)S(1)}, u32[]{:S(2)}, u32[]{:S(2)}) collective-permute-start(bf16[128,2048]{1,0:T(8,128)(2,1)} %get-tuple-element.69), channel_id=1, source_target_pairs={{0,64},{32,96},{64,0},{96,32},{1,65},{33,97},{65,1},{97,33},{2,66}... | collective-permute-start | bytes 1572872 | tf_op jit(solution)/shard_map/ppermute | solution.py:34
  269.2 31.3 %collective-permute-start.37 = (bf16[128,2048]{1,0:T(8,128)(2,1)S(1)}, bf16[128,2048]{1,0:T(8,128)(2,1)S(1)}, u32[]{:S(2)}, u32[]{:S(2)}) collective-permute-start(bf16[128,2048]{1,0:T(8,128)(2,1)S(1)} %get-tuple-element.70), channel_id=1, source_target_pairs={{0,96},{32,0},{64,32},{96,64},{1,97},{33,1},{65,33},{97,65},{2,98}... | collective-permute-start | bytes 1572872 | tf_op jit(solution)/shard_map/ppermute | solution.py:34
  270.9 29.6 %collective-permute-start.36 = (bf16[128,2048]{1,0:T(8,128)(2,1)S(1)}, bf16[128,2048]{1,0:T(8,128)(2,1)S(1)}, u32[]{:S(2)}, u32[]{:S(2)}) collective-permute-start(bf16[128,2048]{1,0:T(8,128)(2,1)S(1)} %get-tuple-element.71), channel_id=1, source_target_pairs={{0,32},{32,64},{64,96},{96,0},{1,33},{33,65},{65,97},{97,1},{2,34}... | collective-permute-start | bytes 1572872 | tf_op jit(solution)/shard_map/ppermute | solution.py:34
  317.8 19.8 %collective-permute-start.46 = (bf16[16,64,1152]{2,1,0:T(8,128)(2,1)}, bf16[16,64,1152]{2,1,0:T(8,128)(2,1)}, u32[]{:S(2)}, u32[]{:S(2)}) collective-permute-start(bf16[16,64,1152]{2,1,0:T(8,128)(2,1)} %dynamic-slice_bitcast_fusion), channel_id=1, source_target_pairs={{0,1},{1,0},{2,3},{3,2},{4,5},{5,4},{6,7},{7,6},{8,9},{9,8},{10,11... | collective-permute-start | bytes 7077896 | tf_op jit(solution)/shard_map/ppermute | solution.py:34
  325.6 18.1 %collective-permute-start.43 = (bf16[64,2048]{1,0:T(8,128)(2,1)S(1)}, bf16[64,2048]{1,0:T(8,128)(2,1)S(1)}, u32[]{:S(2)}, u32[]{:S(2)}) collective-permute-start(bf16[64,2048]{1,0:T(8,128)(2,1)S(1)} %get-tuple-element.67), channel_id=1, source_target_pairs={{0,32},{32,64},{64,96},{96,0},{1,33},{33,65},{65,97},{97,1},{2,34}... | collective-permute-start | bytes 786440 | tf_op jit(solution)/shard_map/ppermute | solution.py:34
  326.0 17.9 %collective-permute-start.42 = (bf16[64,2048]{1,0:T(8,128)(2,1)S(1)}, bf16[64,2048]{1,0:T(8,128)(2,1)S(1)}, u32[]{:S(2)}, u32[]{:S(2)}) collective-permute-start(bf16[64,2048]{1,0:T(8,128)(2,1)S(1)} %get-tuple-element.68), channel_id=1, source_target_pairs={{0,96},{32,0},{64,32},{96,64},{1,97},{33,1},{65,33},{97,65},{2,98}... | collective-permute-start | bytes 786440 | tf_op jit(solution)/shard_map/ppermute | solution.py:34
  334.3 13.5 %collective-permute-start.41 = (bf16[64,2048]{1,0:T(8,128)(2,1)S(1)}, bf16[64,2048]{1,0:T(8,128)(2,1)S(1)}, u32[]{:S(2)}, u32[]{:S(2)}) collective-permute-start(bf16[64,2048]{1,0:T(8,128)(2,1)S(1)} %get-tuple-element.63), channel_id=1, source_target_pairs={{0,32},{32,64},{64,96},{96,0},{1,33},{33,65},{65,97},{97,1},{2,34}... | collective-permute-start | bytes 786440 | tf_op jit(solution)/shard_map/ppermute | solution.py:34
  340.5 17.7 %collective-permute-start.48 = (bf16[272,1152]{1,0:T(8,128)(2,1)S(1)}, bf16[272,1152]{1,0:T(8,128)(2,1)S(1)}, u32[]{:S(2)}, u32[]{:S(2)}) collective-permute-start(bf16[272,1152]{1,0:T(8,128)(2,1)S(1)} %get-tuple-element.112), channel_id=1, source_target_pairs={{0,2},{2,4},{4,6},{6,0},{1,3},{3,5},{5,7},{7,1},{8,10},{10,12},{12... | collective-permute-start | bytes 1880072 | tf_op jit(solution)/shard_map/ppermute | solution.py:34
  343.7 17.1 %collective-permute-start.49 = (bf16[272,1152]{1,0:T(8,128)(2,1)S(1)}, bf16[272,1152]{1,0:T(8,128)(2,1)S(1)}, u32[]{:S(2)}, u32[]{:S(2)}) collective-permute-start(bf16[272,1152]{1,0:T(8,128)(2,1)S(1)} %get-tuple-element.113), channel_id=1, source_target_pairs={{0,6},{2,0},{4,2},{6,4},{1,7},{3,1},{5,3},{7,5},{8,14},{10,8},{12,... | collective-permute-start | bytes 1880072 | tf_op jit(solution)/shard_map/ppermute | solution.py:34
  343.9 28.1 %collective-permute-start.50 = (bf16[272,1152]{1,0:T(8,128)(2,1)S(1)}, bf16[272,1152]{1,0:T(8,128)(2,1)S(1)}, u32[]{:S(2)}, u32[]{:S(2)}) collective-permute-start(bf16[272,1152]{1,0:T(8,128)(2,1)S(1)} %get-tuple-element.114), channel_id=1, source_target_pairs={{0,4},{2,6},{4,0},{6,2},{1,5},{3,7},{5,1},{7,3},{8,12},{10,14},{12... | collective-permute-start | bytes 1880072 | tf_op jit(solution)/shard_map/ppermute | solution.py:34
  (54 other events, 437.8 us)
Sparse Core Ops, SparseCore 0:
  10.8 49.1 all-gather.2
  62.3 75.5 all-gather.4
  206.0 115.4 reduce-scatter.1
